TPU v7x, 512 devices: a whole 4x4x16 slice. The times are simulated.
512 devices in a mesh: lon: 64 (over x_hi, z, core), lat: 8 (over x_lo, y).
Axes of the slice: x: 4 (x_hi: 2, x_lo: 2; x = x_hi * 2 + x_lo), y: 4, z: 16, core: 2. Of those that a mesh axis runs over, the one named last changes fastest.
Arguments:
- tokens: bfloat16 [2, 48, 768, 512], P(None, 'lat', 'lon'), may hold values from -16 to 16
- key_valid: int32 [2, 48, 768], P(None, 'lat', 'lon'), may hold values 0 or 1
- norm_gain: float32 [512], replicated, may hold values from 0.5 to 1.5
- w_qkv: bfloat16 [512, 1536], replicated, may hold values from -0.25 to 0.25
- bias_table: float32 [8, 759], replicated, may hold values from -4 to 4
- w_proj: bfloat16 [512, 512], replicated, may hold values from -0.25 to 0.25
- grad_out: bfloat16 [2, 48, 768, 512], P(None, 'lat', 'lon'), may hold values from -6 to 6
Outputs:
- result: bfloat16 [2, 48, 768, 512], P(None, 'lat', 'lon')
- grad_in: bfloat16 [2, 48, 768, 512], P(None, 'lat', 'lon')
- grad_qkv: float32 [512, 1536], P(('lon', 'lat'))
- grad_gain: float32 [512], replicated
- grad_bias: float32 [8, 759], replicated
All inputs are finite; a program needn't handle non-finite values. No bound on the sum of `key_valid` on one device may be relied on, other than what follows from the above.
Results may differ from a plain program's by a relative error of at most 0.014.
Values may be sent and summed in bfloat16 or wider, within the bound.
A program may use at most 64 MiB of HBM per device.

v0:
```python
from functools import partial

import jax
import jax.numpy as jnp
from jax import lax
from jax.sharding import PartitionSpec as P

LEVELS = 2
WLAT = 6
WLON = 12


def as_sent(x):

    def short(part):
        return part.astype(jnp.bfloat16) if part.dtype == jnp.float32 else part

    return jax.tree.map(short, x)


def from_behind(x, axis, by):
    size = lax.axis_size(axis)
    return lax.ppermute(x, axis, [(i, (i + by) % size) for i in range(size)])


def layer_norm(values, norm_gain):
    centred = values - jnp.mean(values, axis=-1, keepdims=True)
    spread = jnp.mean(centred * centred, axis=-1, keepdims=True)
    return (centred * lax.rsqrt(spread + 1e-05) * norm_gain).astype(jnp.bfloat16)


def relative_index():
    window_size = LEVELS * WLAT * WLON
    places = jnp.arange(window_size, dtype=jnp.int32)
    level_pos = places // (WLAT * WLON)
    row_pos = places // WLON % WLAT
    col_pos = places % WLON
    level_gap = level_pos[:, None] - level_pos[None, :] + (LEVELS - 1)
    row_gap = row_pos[:, None] - row_pos[None, :] + (WLAT - 1)
    col_gap = col_pos[:, None] - col_pos[None, :] + (WLON - 1)
    return (level_gap * (2 * WLAT - 1) + row_gap) * (2 * WLON - 1) + col_gap


def allowance(region, key_mask):
    window_size = region.shape[1]
    same_region = (region[:, :, None] == region[:, None, :]).astype(jnp.float32)
    self_mask = jnp.eye(window_size, dtype=jnp.float32)
    return same_region * jnp.maximum(key_mask[:, None, :], self_mask[None])


def attend(qkv_act, bias_table, allowed, rel_index):
    window_count, window_size, triple = qkv_act.shape
    head_count = bias_table.shape[0]
    head_size = triple // (3 * head_count)
    pieces = qkv_act.reshape(window_count, window_size, 3, head_count, head_size)
    scores = jnp.einsum(
        "wqhd,wkhd->whqk", pieces[:, :, 0], pieces[:, :, 1], preferred_element_type=jnp.float32
    )
    scores = scores * head_size ** (-0.5) + jnp.take(bias_table, rel_index, axis=1)[None]
    weights = jnp.exp(scores) * allowed[:, None]
    attention = (weights / jnp.sum(weights, axis=-1, keepdims=True)).astype(jnp.bfloat16)
    mixed = jnp.einsum(
        "whqk,wkhd->wqhd", attention, pieces[:, :, 2], preferred_element_type=jnp.float32
    )
    return mixed.astype(jnp.bfloat16).reshape(window_count * window_size, head_count * head_size)


def window_pass(windows, allowed, w_qkv, bias_table, w_proj, rel_index, cot_windows):
    window_count, window_size, feature_width = windows.shape
    flat_rows = windows.reshape(window_count * window_size, feature_width)
    qkv_act = jnp.dot(flat_rows, w_qkv, preferred_element_type=jnp.float32).astype(jnp.bfloat16)
    mixed, pullback = jax.vjp(
        partial(attend, allowed=allowed, rel_index=rel_index),
        qkv_act.reshape(window_count, window_size, -1),
        bias_table,
    )
    attn_out = jnp.dot(mixed, w_proj, preferred_element_type=jnp.float32).astype(jnp.bfloat16)
    cot_rows = cot_windows.reshape(window_count * window_size, feature_width)
    grad_mixed = lax.dot_general(
        cot_rows, w_proj, (((1,), (1,)), ((), ())), preferred_element_type=jnp.float32
    ).astype(jnp.bfloat16)
    grad_act, grad_table = pullback(grad_mixed)
    grad_act = grad_act.reshape(window_count * window_size, -1)
    grad_rows = lax.dot_general(
        grad_act, w_qkv, (((1,), (1,)), ((), ())), preferred_element_type=jnp.float32
    ).astype(jnp.bfloat16)
    grad_weight = lax.dot_general(
        flat_rows, grad_act, (((0,), (0,)), ((), ())), preferred_element_type=jnp.float32
    )
    return (
        attn_out.reshape(windows.shape),
        grad_rows.reshape(windows.shape),
        grad_weight,
        grad_table,
    )


def to_windows(grid):
    levels, row_count, col_count = grid.shape[:3]
    trailing = grid.shape[3:]
    split_grid = grid.reshape((levels, row_count // WLAT, WLAT, col_count // WLON, WLON) + trailing)
    axis_order = (3, 1, 0, 2, 4) + tuple(range(5, 5 + len(trailing)))
    return split_grid.transpose(axis_order).reshape(
        (col_count // WLON, row_count // WLAT, levels * WLAT * WLON) + trailing
    )


def from_windows(blocks, levels):
    col_blocks, row_blocks = blocks.shape[:2]
    trailing = blocks.shape[3:]
    split_grid = blocks.reshape((col_blocks, row_blocks, levels, WLAT, WLON) + trailing)
    axis_order = (2, 1, 3, 0, 4) + tuple(range(5, 5 + len(trailing)))
    return split_grid.transpose(axis_order).reshape(
        (levels, row_blocks * WLAT, col_blocks * WLON) + trailing
    )


def along_lon(pieces, offset):
    return jax.tree.map(
        lambda part, own: part.astype(own.dtype),
        from_behind(as_sent(pieces), "lon", offset),
        pieces,
    )


def along_lat(pieces, offset):
    return jax.tree.map(
        lambda part, own: part.astype(own.dtype),
        from_behind(as_sent(pieces), "lat", offset),
        pieces,
    )


def fetch(pieces):
    half_lat = WLAT // 2
    half_lon = WLON // 2
    arrived = along_lon(tuple((piece[:, :, :half_lon] for piece in pieces)), -1)
    widened = tuple(
        (jnp.concatenate([piece, extra], axis=2) for piece, extra in zip(pieces, arrived))
    )
    rim_rows = along_lat(tuple((piece[:, :half_lat, half_lon:] for piece in widened)), -1)
    return tuple(
        (
            jnp.concatenate([piece[:, half_lat:, half_lon:], extra], axis=1)
            for piece, extra in zip(widened, rim_rows)
        )
    )


def restore(blocks):
    half_lat = WLAT // 2
    half_lon = WLON // 2
    row_count, col_count = (blocks[0].shape[1], blocks[0].shape[2])
    tail_rows = along_lat(tuple((block[:, row_count - half_lat :] for block in blocks)), 1)
    blocks = tuple(
        (
            jnp.concatenate([tail, block[:, : row_count - half_lat]], axis=1)
            for tail, block in zip(tail_rows, blocks)
        )
    )
    tail_cols = along_lon(tuple((block[:, :, col_count - half_lon :] for block in blocks)), 1)
    return tuple(
        (
            jnp.concatenate([tail, block[:, :, : col_count - half_lon]], axis=2)
            for tail, block in zip(tail_cols, blocks)
        )
    )


def local(tokens, key_valid, norm_gain, w_qkv, bias_table, w_proj, grad_out):
    levels, row_count, col_count, feature_width = tokens.shape
    half_lat = WLAT // 2
    values = tokens.astype(jnp.float32)
    normed, norm_pullback = jax.vjp(layer_norm, values, norm_gain)
    shifted, mask_shift = fetch((normed, key_valid.astype(jnp.bfloat16)))
    cot_shift = fetch((grad_out,))[0]
    lat_devices = lax.axis_size("lat")
    row_global = (
        row_count * lax.axis_index("lat") + half_lat + jnp.arange(row_count, dtype=jnp.int32)
    ) % (row_count * lat_devices)
    region = jnp.broadcast_to(
        (row_global < half_lat).astype(jnp.int32)[None, :, None], (levels, row_count, col_count)
    )
    blocks = to_windows(shifted)
    col_blocks, row_blocks, window_size = blocks.shape[:3]
    window_count = col_blocks * row_blocks
    allowed = allowance(
        to_windows(region).reshape(window_count, window_size),
        to_windows(mask_shift.astype(jnp.float32)).reshape(window_count, window_size),
    )
    attn_out, grad_rows, grad_weight, grad_table = window_pass(
        blocks.reshape(window_count, window_size, feature_width),
        allowed,
        w_qkv,
        bias_table,
        w_proj,
        relative_index(),
        to_windows(cot_shift).reshape(window_count, window_size, feature_width),
    )
    grad_qkv = lax.psum_scatter(grad_weight, ("lon", "lat"), scatter_dimension=0, tiled=True)
    attn_block = from_windows(
        attn_out.reshape(col_blocks, row_blocks, window_size, feature_width), levels
    )
    grad_block = from_windows(
        grad_rows.reshape(col_blocks, row_blocks, window_size, feature_width), levels
    )
    attention_grid = restore((attn_block,))[0]
    grad_normed = restore((grad_block,))[0]
    result = (values + attention_grid.astype(jnp.float32)).astype(jnp.bfloat16)
    grad_values, gain_local = norm_pullback(grad_normed)
    grad_in = (grad_out.astype(jnp.float32) + grad_values).astype(jnp.bfloat16)
    grad_gain, grad_bias = lax.psum((gain_local, grad_table), ("lon", "lat"))
    return (result, grad_in, grad_qkv, grad_gain, grad_bias)


def solution(mesh):
    placed = (
        P(None, "lat", "lon", None),
        P(None, "lat", "lon"),
        P(),
        P(),
        P(),
        P(),
        P(None, "lat", "lon", None),
    )
    return jax.shard_map(
        local,
        mesh=mesh,
        in_specs=placed,
        out_specs=(
            P(None, "lat", "lon", None),
            P(None, "lat", "lon", None),
            P(("lon", "lat"), None),
            P(),
            P(),
        ),
        check_vma=False,
    )
```

profile of v0, /device:TPU:1, one launch (start us, length us, event | category | flops | bytes accessed | tf_op | source)
XLA Modules:
  0.0 611.6 jit_solution(18098207350715541206)
XLA Ops:
  7.2 1.1 convert_reduce_fusion
  8.4 1.1 fusion.22
  9.5 1.1 fusion.20
  10.6 8.8 %collective-permute-start = (bf16[2,6,6,512]{3,2,1,0:T(8,128)(2,1)S(1)}, bf16[2,6,6,512]{3,2,1,0:T(8,128)(2,1)S(1)}, u32[]{:S(2)}, u32[]{:S(2)}) collective-permute-start(bf16[2,6,6,512]{3,2,1,0:T(8,128)(2,1)S(1)} %slice.82), channel_id=1, source_target_pairs={{0,504},{8,0},{16,8},{24,16},{32,24},{40,32},{48,40},{56,48},{64,5... | collective-permute-start | bytes 221192 | tf_op jit(solution)/shard_map/ppermute | solution.py:23
  19.4 0.7 convert_element_type.115
  20.1 7.9 %collective-permute-start.2 = (bf16[2,6,6]{2,0,1:T(2,128)(2,1)S(1)}, bf16[2,6,6]{2,0,1:T(2,128)(2,1)S(1)}, u32[]{:S(2)}, u32[]{:S(2)}) collective-permute-start(bf16[2,6,6]{2,0,1:T(2,128)(2,1)S(1)} %bitcast.80), channel_id=1, source_target_pairs={{0,504},{8,0},{16,8},{24,16},{32,24},{40,32},{48,40},{56,48},{64,5... | collective-permute-start | bytes 440 | tf_op jit(solution)/shard_map/ppermute | solution.py:23
  28.0 0.9 slice.73
  29.0 2.6 collective-permute-start.6
  31.6 0.1 compare_select_fusion
  31.8 0.8 compare_and_fusion
  32.5 0.1 constant_dynamic-update-slice_fusion.1
  32.7 0.1 broadcast_in_dim.32
  32.7 0.1 eq.34
  32.8 0.2 copy.51
  33.0 0.1 reshape.524
  33.2 38.8 %gather_fusion = f32[20736,8]{1,0:T(8,128)} fusion(f32[8,759]{0,1:T(8,128)S(1)} %copy.51, s32[21504]{0:T(1024)S(1)} %pad_clamp_fusion), kind=kCustom, calls=%fused_computation | custom fusion | bytes 1410048 | tf_op jit(solution)/shard_map/jvp(jit(_take))/gather | solution.py:59
  72.0 11.7 %copy.53 = f32[144,144,8]{0,1,2:T(8,128)} copy(f32[144,144,8]{2,1,0:T(8,128)} %bitcast.69) | data formatting | bytes 1327104 | tf_op jit(solution)/shard_map/jvp(jit(_take))/gather | solution.py:59
  83.7 0.1 fusion.34
  83.8 4.7 collective-permute-start.3
  88.5 0.7 collective-permute-done.3
  89.2 0.1 reshape.521
  89.3 0.8 maximum_select_fusion
  90.1 5.7 collective-permute-start.1
  95.9 0.8 fusion.43
  96.7 1.9 collective-permute-start.7
  98.7 0.6 copy-done.6
  99.4 0.4 convolution_convert_fusion
  99.8 0.3 copy.75
  100.1 1.8 multiply_reduce_fusion
  101.9 0.6 multiply_divide_fusion
  102.5 1.1 pad_maximum_fusion.3
  103.6 0.7 copy.57
  104.3 1.6 reshape_reshape_reshape_transpose_reshape.7
  106.0 2.1 convolution_convert_fusion.7
  108.1 1.8 reshape.518
  109.9 1.9 copy.58
  111.8 1.5 fusion.6
  113.3 0.4 fusion.9
  113.7 0.4 fusion.8
  114.2 1.4 fusion.41
  115.6 0.3 fusion.7
  115.9 1.0 convolution_convert_fusion.5
  116.8 0.2 pad_add_fusion
  117.0 0.7 convolution_convert_fusion.6
  117.7 0.2 copy-done.7
  117.9 2.4 fusion.46
  120.4 0.7 fusion.44
  121.1 3.5 collective-permute-start.8
  124.6 1.3 convolution_convert_fusion.8
  126.0 2.1 collective-permute-start.4
  128.1 10.0 %copy.74 = f32[144,144,8]{2,1,0:T(8,128)} copy(f32[144,144,8]{0,1,2:T(8,128)S(1)} %copy-done.2) | data formatting | bytes 1327104 | tf_op jit(solution)/shard_map/transpose(jvp())/mul | solution.py:60
  138.1 112.5 %scatter_custom_fusion = f32[8,759]{0,1:T(8,128)S(1)} fusion(s32[20736]{0:T(1024)} %copy-done.10, f32[20736,8]{1,0:T(8,128)} %bitcast.70, f32[]{:T(128)} %constant.73.clone.1), kind=kCustom, calls=%fused_computation.65 | custom fusion | flops 165888 | bytes 24800 | tf_op jit(solution)/shard_map/transpose(jvp(jit(_take)))/scatter-add | solution.py:59
  250.7 0.9 fusion.31
  251.6 5.0 collective-permute-start.9
  256.7 1.9 collective-permute-start.5
  258.6 1.1 fusion.23
  259.8 1.2 fusion.21
  261.1 1.2 add_convert_fusion
  262.3 0.8 copy.65
  263.1 0.8 copy.66
  263.9 108.7 %all-reduce.4 = (f32[512]{0:T(512)}, f32[8,759]{0,1:T(8,128)S(1)}) all-reduce(f32[512]{0:T(512)S(1)} %get-tuple-element.20, f32[8,759]{0,1:T(8,128)S(1)} %scatter_custom_fusion), channel_id=1, replica_groups=mesh['lon'=64,'lat'=8] {'lon','lat'}, use_global_device_ids=true, to_apply=%region_8.9 | all-reduce | flops 6584 | bytes 52672 | tf_op jit(solution)/shard_map/psum | solution.py:212
  372.6 0.7 copy.67
  373.4 230.0 %all-reduce.7.cloned.1.call-done = f32[512,1536]{1,0:T(8,128)} async-done(((f32[512,1536]{1,0:T(8,128)}), f32[512,1536]{1,0:T(8,128)}) %all-reduce.7.cloned.1.call-update) | async-done | bytes 3145744
  603.4 1.4 constant_dynamic-slice_fusion
  (65 shorter events, 0.6 us)
Async XLA Ops:
  7.2 92.2 %copy-start = (bf16[512,1536]{1,0:T(8,128)(2,1)S(1)}, bf16[512,1536]{1,0:T(8,128)(2,1)}, u32[]{:S(2)}) copy-start(bf16[512,1536]{1,0:T(8,128)(2,1)} %param.10) | copy-start | bytes 4718596
  7.2 25.4 %copy-start.8 = (bf16[2,6,12,512]{3,0,2,1:T(2,128)(2,1)S(1)}, bf16[2,6,12,512]{3,0,2,1:T(2,128)(2,1)}, u32[]{:S(2)}) copy-start(bf16[2,6,12,512]{3,0,2,1:T(2,128)(2,1)} %param.13) | copy-start | bytes 442372
  7.2 25.6 %copy-start.17 = (f32[8,759]{1,0:T(8,128)S(1)}, f32[8,759]{1,0:T(8,128)}, u32[]{:S(2)}) copy-start(f32[8,759]{1,0:T(8,128)} %param.11) | copy-start | bytes 72868
  7.2 596.2 %all-reduce.7.cloned.1.call-start = ((), (), s32[]{:S(2)}) async-start(), calls=%async_computation | async-start | bytes 6291456
  9.5 23.2 %copy-start.14 = (f32[2,6,12]{2,1,0:T(8,128)}, f32[2,6,12]{2,1,0:T(8,128)S(1)}, u32[]{:S(2)}) copy-start(f32[2,6,12]{2,1,0:T(8,128)S(1)} %fusion.22) | copy-start | bytes 1732
  10.6 79.4 %collective-permute-start = (bf16[2,6,6,512]{3,2,1,0:T(8,128)(2,1)S(1)}, bf16[2,6,6,512]{3,2,1,0:T(8,128)(2,1)S(1)}, u32[]{:S(2)}, u32[]{:S(2)}) collective-permute-start(bf16[2,6,6,512]{3,2,1,0:T(8,128)(2,1)S(1)} %slice.82), channel_id=1, source_target_pairs={{0,504},{8,0},{16,8},{24,16},{32,24},{40,32},{48,40},{56,48},{64,5... | collective-permute-start | bytes 221192 | tf_op jit(solution)/shard_map/ppermute | solution.py:23
  20.1 63.6 %collective-permute-start.2 = (bf16[2,6,6]{2,0,1:T(2,128)(2,1)S(1)}, bf16[2,6,6]{2,0,1:T(2,128)(2,1)S(1)}, u32[]{:S(2)}, u32[]{:S(2)}) collective-permute-start(bf16[2,6,6]{2,0,1:T(2,128)(2,1)S(1)} %bitcast.80), channel_id=1, source_target_pairs={{0,504},{8,0},{16,8},{24,16},{32,24},{40,32},{48,40},{56,48},{64,5... | collective-permute-start | bytes 440 | tf_op jit(solution)/shard_map/ppermute | solution.py:23
  29.0 66.8 %collective-permute-start.6 = (bf16[2,6,6,512]{3,0,2,1:T(2,128)(2,1)S(1)}, bf16[2,6,6,512]{3,0,2,1:T(2,128)(2,1)S(1)}, u32[]{:S(2)}, u32[]{:S(2)}) collective-permute-start(bf16[2,6,6,512]{3,0,2,1:T(2,128)(2,1)S(1)} %slice.73), channel_id=1, source_target_pairs={{0,504},{8,0},{16,8},{24,16},{32,24},{40,32},{48,40},{56,48},{64,5... | collective-permute-start | bytes 221192 | tf_op jit(solution)/shard_map/ppermute | solution.py:23
  33.1 38.9 %copy-start.10 = (s32[20736]{0:T(1024)}, s32[20736]{0:T(1024)S(1)}, u32[]{:S(2)}) copy-start(s32[20736]{0:T(1024)S(1)} %reshape.524) | copy-start | bytes 248836
  83.8 5.4 collective-permute-start.3
  90.1 8.5 %collective-permute-start.1 = (bf16[2,3,12,512]{3,2,1,0:T(8,128)(2,1)S(1)}, bf16[2,3,12,512]{3,2,1,0:T(8,128)(2,1)S(1)}, u32[]{:S(2)}, u32[]{:S(2)}) collective-permute-start(bf16[2,3,12,512]{3,2,1,0:T(8,128)(2,1)S(1)} %pad_maximum_fusion.4), channel_id=1, source_target_pairs={{0,7},{1,0},{2,1},{3,2},{4,3},{5,4},{6,5},{7,6},{8,15},{9,8},{10,9... | collective-permute-start | bytes 221192 | tf_op jit(solution)/shard_map/ppermute | solution.py:23
  96.7 5.9 collective-permute-start.7
  98.7 0.7 copy-start.6
  100.1 2.5 copy-start.11
  101.9 1.7 copy-start.12
  111.8 1.5 copy-start.3
  111.8 1.5 copy-start.13
  114.2 1.4 copy-start.4
  117.0 0.9 copy-start.7
  121.1 3.5 copy-start.5
  121.1 129.6 %collective-permute-start.8 = (bf16[2,3,12,512]{3,2,1,0:T(8,128)(2,1)}, bf16[2,3,12,512]{3,2,1,0:T(8,128)(2,1)}, u32[]{:S(2)}, u32[]{:S(2)}) collective-permute-start(bf16[2,3,12,512]{3,2,1,0:T(8,128)(2,1)} %get-tuple-element.28), channel_id=1, source_target_pairs={{0,1},{1,2},{2,3},{3,4},{4,5},{5,6},{6,7},{7,0},{8,9},{9,10},{10,1... | collective-permute-start | bytes 221192 | tf_op jit(solution)/shard_map/ppermute | solution.py:23
  124.6 3.5 copy-start.2
  126.0 130.6 %collective-permute-start.4 = (bf16[2,3,12,512]{3,2,1,0:T(8,128)(2,1)S(1)}, bf16[2,3,12,512]{3,2,1,0:T(8,128)(2,1)S(1)}, u32[]{:S(2)}, u32[]{:S(2)}) collective-permute-start(bf16[2,3,12,512]{3,2,1,0:T(8,128)(2,1)S(1)} %get-tuple-element.30), channel_id=1, source_target_pairs={{0,1},{1,2},{2,3},{3,4},{4,5},{5,6},{6,7},{7,0},{8,9},{9,10},{10,1... | collective-permute-start | bytes 221192 | tf_op jit(solution)/shard_map/ppermute | solution.py:23
  128.1 130.5 %copy-start.1 = (bf16[2,6,12,512]{3,0,2,1:T(2,128)(2,1)S(1)}, bf16[2,6,12,512]{3,0,2,1:T(2,128)(2,1)}, u32[]{:S(2)}) copy-start(bf16[2,6,12,512]{3,0,2,1:T(2,128)(2,1)} %param.7) | copy-start | bytes 442372
  128.1 130.5 %copy-start.16 = (f32[512]{0:T(512)S(1)}, f32[512]{0:T(512)}, u32[]{:S(2)}) copy-start(f32[512]{0:T(512)} %param.9) | copy-start | bytes 6148
  138.1 121.7 %copy-start.15 = (f32[2,6,12]{2,1,0:T(8,128)S(1)}, f32[2,6,12]{2,1,0:T(8,128)}, u32[]{:S(2)}) copy-start(f32[2,6,12]{2,1,0:T(8,128)} %copy-done.14) | copy-start | bytes 1732
  138.1 123.0 %copy-start.9 = (bf16[2,6,12,512]{3,0,2,1:T(2,128)(2,1)S(1)}, bf16[2,6,12,512]{3,0,2,1:T(2,128)(2,1)}, u32[]{:S(2)}) copy-start(bf16[2,6,12,512]{3,0,2,1:T(2,128)(2,1)} %param.13) | copy-start | bytes 442372
  251.6 7.0 %collective-permute-start.9 = (bf16[2,6,6,512]{3,2,1,0:T(8,128)(2,1)S(1)}, bf16[2,6,6,512]{3,2,1,0:T(8,128)(2,1)S(1)}, u32[]{:S(2)}, u32[]{:S(2)}) collective-permute-start(bf16[2,6,6,512]{3,2,1,0:T(8,128)(2,1)S(1)} %fusion.31), channel_id=1, source_target_pairs={{0,8},{8,16},{16,24},{24,32},{32,40},{40,48},{48,56},{56,64},{64,7... | collective-permute-start | bytes 221192 | tf_op jit(solution)/shard_map/ppermute | solution.py:23
  256.7 4.4 collective-permute-start.5
Sparse Core Ops, SparseCore 0:
  124.7 478.6 all-reduce.6
where the time goes:
time: 613 us; the launch traced here: 612 us
  waiting for transfers between devices  231 us (38%)
  other arithmetic  126 us (21%)
  blocking collectives  109 us (18%)
  local copies, waits for them, and re-layouts  74.7 us (12%)
  starting transfers between devices  44.1 us (7%)
  between operations  14.7 us (2%)
  matrix products  12.3 us (2%)
    unnamed x2, waiting for transfers between devices  230 us
    scatter-add x1, other arithmetic, attend(): jnp.take(bias_table, rel_index, axis=1)[None]  113 us
    psum x1, blocking collectives, local(): grad_gain, grad_bias = lax.psum((gain_local, grad_table), ('lon', 'lat'))  109 us
    gather x2, local copies, waits for them, and re-layouts, attend(): jnp.take(bias_table, rel_index, axis=1)[None]  50.5 us
    ppermute x10, starting transfers between devices, from_behind(): return lax.ppermute(x, axis, [(i, (i + by) % size) for i in range(size)])  44 us
  transfers between devices with their start and end apart: 11, of which 2 were waited for; matrix products, arithmetic and copies ran while one was open for 31% of the time, Pallas kernels for 0%

commit v1 on v0

v1 whole, which is shorter than its diff:
```python
import jax
import jax.numpy as jnp
import numpy as np
from jax import lax
from jax.experimental import pallas as pl
from jax.experimental.pallas import tpu as pltpu
from jax.sharding import PartitionSpec as P

MESH = pl.DeviceIdType.MESH
F32 = jnp.float32
BF16 = jnp.bfloat16

LEVELS, WLAT, WLON = 2, 6, 12
WIN = LEVELS * WLAT * WLON
D = 512
HEADS = 8
PAIRS = HEADS // 2
RELN = 759
RELP = 768
N_LON, N_LAT = 64, 8
N_Z = 16
N_PLANE = 16
MSG = 80
CHUNK = 3 * 128


def offset_of(t):
    level, row, col = t // 72, t // 12 % 6, t % 12
    return 253 * level + 23 * row + col


def make_tables():
    pack = np.zeros((4 * MSG, 2 * 192), np.float32)
    unpack = np.zeros((304, 4 * MSG), np.float32)
    key_col = np.zeros((128, D), np.float32)
    key_row = np.zeros((4, 16, D), np.float32)
    for l in range(LEVELS):
        for r in range(WLAT):
            for c in range(WLON):
                quad = (r // 3) * 2 + c // 6
                place = l * 18 + (r % 3) * 6 + c % 6
                t = WIN - 1 - (l * 72 + ((r + 3) % 6) * 12 + (c + 6) % 12)
                for a in range(2):
                    msg = quad * MSG + a * 36 + place
                    pack[msg, a * 192 + (l * 6 + r) * 16 + c] = 1
                    unpack[a * WIN + t, msg] = 1
                key_col[c, t] = 1
                key_row[quad, l * 8 + r, t] = 1
    for quad in range(4):
        unpack[2 * WIN, quad * MSG + 72] = 1
    perm = np.zeros((D, D), np.float32)
    for core in range(2):
        for xh in range(2):
            for lat in range(8):
                for z in range(16):
                    perm[core * 256 + (xh * 8 + lat) * 16 + z, xh * 256 + z * 16 + core * 8 + lat] = 1
    pick = np.zeros((6, WIN, RELP), np.float32)
    for g in range(6):
        for k in range(WIN):
            pick[g, k, (379 + offset_of(k) - 253 * (g // 3) - 46 * (g % 3)) % RELP] = 1
    step = np.arange(24)
    step = np.tile(23 * (step // 12) + step % 12, HEADS)
    skew = np.broadcast_to(step[:, None], (192, 128)).astype(np.int32)
    t = np.arange(WIN)
    half = ((WIN - 1 - t) // 12 % 6) >= 3
    masks = np.stack([half[:, None] != half[None, :], np.eye(WIN, dtype=bool)]).astype(np.float32)
    as_bf16 = lambda v: jnp.asarray(v, BF16)
    return (
        as_bf16(pack),
        as_bf16(unpack),
        as_bf16(pack.T),
        as_bf16(unpack[: 2 * WIN].T),
        as_bf16(key_col),
        jnp.asarray(key_row),
        as_bf16(perm),
        as_bf16(pick),
        jnp.asarray(skew),
        jnp.asarray(masks),
    )


def dot(a, b):
    return lax.dot_general(a, b, (((1,), (0,)), ((), ())), preferred_element_type=F32)


def dot_nt(a, b):
    return lax.dot_general(a, b, (((1,), (1,)), ((), ())), preferred_element_type=F32)


def dot_tn(a, b):
    return lax.dot_general(a, b, (((0,), (0,)), ((), ())), preferred_element_type=F32)


def skewed(rows, skew, left):
    for bit in (1, 2, 4, 8, 16, 32):
        moved = pltpu.roll(rows, RELP - bit if left else bit, 1)
        rows = jnp.where((skew & bit) != 0, moved, rows)
    return rows


def kernel(
    tok, kv, gain, w_qkv, table, w_proj, gout,
    pack, unpack, pack_t, unpack_t, key_col, key_row, perm, pick, skew_ref, masks,
    result, grad_in, grad_qkv, grad_gain, grad_bias,
    flat, kvs, tabs, hsend, hrecv, bsend, brecv, bias, allowed, dscore,
    qkvs, gms, mixs, dqkv, s1, r1, s2, r2, s3, r3, ex, exr, exc, rx2, rx3, rx4,
    sem_hs, sem_hr, sem_bs, sem_br, sem_s1, sem_r1, sem_s2, sem_r2, sem_s3, sem_r3, sem_xs, sem_xr,
):
    lon, lat = lax.axis_index("lon"), lax.axis_index("lat")
    xh, zc = lax.div(lon, 32), lax.rem(lon, 32)
    z, core = lax.div(zc, 2), lax.rem(zc, 2)
    plane = xh * 8 + lat
    west, east = lax.rem(lon + N_LON - 1, N_LON), lax.rem(lon + 1, N_LON)
    north, south = lax.rem(lat + N_LAT - 1, N_LAT), lax.rem(lat + 1, N_LAT)
    twin = {"lon": lon + 1 - 2 * core, "lat": lat}
    halo_to = ({"lon": west, "lat": north}, {"lon": lon, "lat": north}, {"lon": west, "lat": lat})
    back_to = ({"lon": east, "lat": south}, {"lon": lon, "lat": south}, {"lon": east, "lat": lat})

    def plane_at(d):
        other = lax.rem(plane + d, N_PLANE)
        return other, {"lon": lax.div(other, 8) * 32 + zc, "lat": lax.rem(other, 8)}

    def z_at(d):
        other = lax.rem(z + d, N_Z)
        return other, {"lon": xh * 32 + other * 2 + core, "lat": lat}

    def send(src, dst, send_sem, recv_sem, to):
        pltpu.make_async_remote_copy(
            src_ref=src, dst_ref=dst, send_sem=send_sem, recv_sem=recv_sem,
            device_id=to, device_id_type=MESH,
        ).start()

    def wait(ref, sem):
        pltpu.make_async_copy(ref, ref, sem).wait()

    barrier = pltpu.get_barrier_semaphore()
    for to in halo_to + back_to + (twin,):
        pl.semaphore_signal(barrier, inc=1, device_id=to, device_id_type=MESH)

    def greet(d, carry):
        pl.semaphore_signal(barrier, inc=1, device_id=plane_at(d)[1], device_id_type=MESH)
        pl.semaphore_signal(barrier, inc=1, device_id=z_at(d)[1], device_id_type=MESH)
        return carry

    lax.fori_loop(1, 16, greet, 0)

    flat[...] = jnp.zeros_like(flat)
    for a, ref in enumerate((tok, gout)):
        for l in range(LEVELS):
            for r in range(WLAT):
                flat[a * 12 + l * 6 + r, 0:WLON, :] = ref[l, r]
    kvs[...] = jnp.zeros_like(kvs)
    for l in range(LEVELS):
        kvs[l * 8 : l * 8 + WLAT, 0:WLON] = kv[l].astype(F32)
    msg = dot(pack[...], flat[...].reshape(2 * 192, D))
    keys = dot(kvs[...].astype(BF16), key_col[...])
    row_at = lax.broadcasted_iota(jnp.int32, (MSG, D), 0)
    for quad in range(4):
        key_line = jnp.sum(keys * key_row[quad], axis=0, keepdims=True)
        block = jnp.where(row_at == 72, key_line, msg[quad * MSG : (quad + 1) * MSG]).astype(BF16)
        if quad == 3:
            hrecv[3] = block
        else:
            hsend[quad] = block

    pl.semaphore_wait(barrier, 37)
    for quad in range(3):
        send(hsend.at[quad], hrecv.at[quad], sem_hs.at[quad], sem_hr.at[quad], halo_to[quad])

    tabs[...] = jnp.zeros_like(tabs)
    tabs[:, 0:RELN] = table[...]
    skew = jnp.broadcast_to(skew_ref[:, 0:1], (192, RELP))
    rows = jnp.concatenate(
        [jnp.broadcast_to(tabs[h : h + 1, :], (24, RELP)) for h in range(HEADS)], axis=0
    )
    rows = skewed(rows, skew, False)
    high = rows.astype(BF16)
    low = (rows - high.astype(F32)).astype(BF16)
    both = jnp.concatenate([high, low], axis=0)
    for g in range(6):
        part = dot_nt(both, pick[g])
        part = part[:192] + part[192:]
        for h in range(HEADS):
            bias[h, g * 24 : (g + 1) * 24, :] = part[h * 24 : (h + 1) * 24]

    for quad in range(3):
        wait(hrecv.at[quad], sem_hr.at[quad])
    window = dot(unpack[...], hrecv[...].reshape(4 * MSG, D))
    x = window[0:WIN]
    cot = window[WIN : 2 * WIN]
    key_ok = window[2 * WIN : 2 * WIN + 1, 0:WIN]
    edge = (lat == N_LAT - 1).astype(F32)
    allowed[...] = (1.0 - edge * masks[0]) * jnp.maximum(key_ok, masks[1])

    centred = x - jnp.mean(x, axis=-1, keepdims=True)
    spread = jnp.mean(centred * centred, axis=-1, keepdims=True)
    rstd = lax.rsqrt(spread + 1e-5)
    xhat = centred * rstd
    normed = (xhat * gain[...]).astype(BF16)
    act = dot(normed, w_qkv[...]).astype(BF16)
    grad_mixed = dot_nt(cot.astype(BF16), w_proj[...]).astype(BF16)
    for j in range(12):
        qkvs[j] = act[:, j * 128 : (j + 1) * 128]
    for j in range(4):
        gms[j] = grad_mixed[:, j * 128 : (j + 1) * 128]
    normed_t = dot_nt(perm[...], normed).astype(BF16)
    first = lax.broadcasted_iota(jnp.int32, (WIN, 128), 1) < 64

    def plane_step(p):
        wait(r1.at[p], sem_r1.at[p])
        s2[p] = (s1[p, core].astype(F32) + r1[p].astype(F32)).astype(BF16).reshape(N_PLANE, N_Z, CHUNK)

        def one(d, carry):
            other, to = plane_at(d)
            send(s2.at[p, other], r2.at[p, d - 1], sem_s2.at[p], sem_r2.at[p], to)
            return carry

        lax.fori_loop(1, N_PLANE, one, 0)

    for p in range(PAIRS):
        q2, k2, v2, gm2 = qkvs[p], qkvs[4 + p], qkvs[8 + p], gms[p]
        zero = jnp.zeros_like(q2)
        mixed = dq = dk = dv = jnp.zeros((WIN, 128), F32)
        for s in range(2):
            h = 2 * p + s
            mine = first if s == 0 else jnp.logical_not(first)
            qm = jnp.where(mine, q2, zero) * jnp.asarray(0.125, BF16)
            km = jnp.where(mine, k2, zero)
            vm = jnp.where(mine, v2, zero)
            gm = jnp.where(mine, gm2, zero)
            weights = jnp.exp(dot_nt(qm, k2) + bias[h]) * allowed[...]
            probs = weights / jnp.sum(weights, axis=-1, keepdims=True)
            attention = probs.astype(BF16)
            mixed = mixed + dot(attention, vm)
            grad_att = dot_nt(gm, v2).astype(BF16).astype(F32)
            pull = probs * grad_att
            grad_scores = pull - probs * jnp.sum(pull, axis=-1, keepdims=True)
            dscore[h] = grad_scores
            short = grad_scores.astype(BF16)
            dq = dq + dot(short, km)
            dk = dk + dot_tn(short, qm)
            dv = dv + dot_tn(attention, gm)
        mixs[:, p * 128 : (p + 1) * 128] = mixed.astype(BF16)
        for j, part in enumerate((dq * 0.125, dk, dv)):
            dqkv[:, j * D + p * 128 : j * D + (p + 1) * 128] = part.astype(BF16)
        act_part = jnp.concatenate([(dq * 0.125).astype(BF16), dk.astype(BF16), dv.astype(BF16)], axis=1)
        s1[p] = dot(normed_t, act_part).astype(BF16).reshape(2, 256, CHUNK)
        send(s1.at[p, 1 - core], r1.at[p], sem_s1.at[p], sem_r1.at[p], twin)
        if p > 0:
            plane_step(p - 1)
    plane_step(PAIRS - 1)

    grad_normed = dot_nt(dqkv[...], w_qkv[...]).astype(BF16).astype(F32)
    grad_hat = grad_normed * gain[...]
    shift = jnp.mean(grad_hat, axis=-1, keepdims=True)
    slope = jnp.mean(grad_hat * xhat, axis=-1, keepdims=True)
    dx = (cot + rstd * (grad_hat - shift - xhat * slope)).astype(BF16)
    out = (x + dot(mixs[...], w_proj[...]).astype(BF16).astype(F32)).astype(BF16)
    back = dot(unpack_t[...], jnp.concatenate([out, dx], axis=0)).astype(BF16)
    for quad in range(3):
        bsend[quad] = back[quad * MSG : (quad + 1) * MSG]
        send(bsend.at[quad], brecv.at[quad], sem_bs.at[quad], sem_br.at[quad], back_to[quad])
    brecv[3] = back[3 * MSG :]

    gain_part = jnp.sum(grad_normed * xhat, axis=0, keepdims=True)
    ex[...] = jnp.zeros_like(ex)
    for j in range(4):
        ex[6, j : j + 1, :] = gain_part[:, j * 128 : (j + 1) * 128]
    table_rows = jnp.zeros((192, RELP), F32)
    for g in range(6):
        group = jnp.concatenate([dscore[h, g * 24 : (g + 1) * 24, :] for h in range(HEADS)], axis=0)
        table_rows = table_rows + dot(group.astype(BF16), pick[g])
    table_rows = skewed(table_rows, skew, True)
    table_part = jnp.sum(table_rows.reshape(HEADS, 24, RELP), axis=1)
    for j in range(6):
        ex[j] = table_part[:, j * 128 : (j + 1) * 128]
    send(ex.at[0:7], exr, sem_xs.at[0], sem_xr.at[0], twin)
    wait(exr, sem_xr.at[0])
    exc[...] = ex[...]
    exc[0:7] = ex[0:7] + exr[...]

    def share_plane(d, carry):
        other, to = plane_at(d)
        send(exc.at[other], rx2.at[d - 1], sem_xs.at[1], sem_xr.at[1], to)
        return carry

    lax.fori_loop(1, N_PLANE, share_plane, 0)
    wait(rx2, sem_xr.at[1])
    rx3[z] = exc[plane] + jnp.sum(rx2[...], axis=0)

    def share_z(d, carry):
        send(rx3.at[z], rx3.at[z], sem_xs.at[2], sem_xr.at[2], z_at(d)[1])
        return carry

    lax.fori_loop(1, N_Z, share_z, 0)

    for p in range(PAIRS):
        wait(r2.at[p], sem_r2.at[p])
        total = s2[p, plane].astype(F32)
        for d in range(N_PLANE - 1):
            total = total + r2[p, d].astype(F32)
        for row in range(N_Z):
            s3[row, :, p * CHUNK : (p + 1) * CHUNK] = total[row : row + 1]

    def spread_z(d, carry):
        other, to = z_at(d)
        send(s3.at[other], r3.at[d - 1], sem_s3, sem_r3, to)
        return carry

    lax.fori_loop(1, N_Z, spread_z, 0)

    wait(rx3.at[0:15], sem_xr.at[2])
    wait(rx3.at[0:15], sem_xs.at[2])
    rx4[plane] = jnp.sum(rx3[...], axis=0)

    def share_back(d, carry):
        send(rx4.at[plane], rx4.at[plane], sem_xs.at[3], sem_xr.at[3], plane_at(d)[1])
        return carry

    lax.fori_loop(1, N_PLANE, share_back, 0)

    for quad in range(3):
        wait(brecv.at[quad], sem_br.at[quad])
    done = dot(pack_t[...], brecv[...].reshape(4 * MSG, D)).astype(BF16)
    for a, ref in enumerate((result, grad_in)):
        for l in range(LEVELS):
            for r in range(WLAT):
                at = (a * 12 + l * 6 + r) * 16
                ref[l, r] = done[at : at + WLON]

    wait(r3, sem_r3)
    line = s3[z] + jnp.sum(r3[...], axis=0)
    for p in range(PAIRS):
        for j in range(3):
            grad_qkv[:, j * D + p * 128 : j * D + (p + 1) * 128] = line[:, p * CHUNK + j * 128 : p * CHUNK + (j + 1) * 128]

    wait(rx4.at[0:15], sem_xr.at[3])
    for j in range(4):
        grad_gain[:, j * 128 : (j + 1) * 128] = rx4[6, j : j + 1, :]
    for j in range(6):
        width = min(128, RELN - j * 128)
        grad_bias[:, j * 128 : j * 128 + width] = rx4[j, :, 0:width]

    for quad in range(3):
        wait(hsend.at[quad], sem_hs.at[quad])
        wait(bsend.at[quad], sem_bs.at[quad])
    for p in range(PAIRS):
        wait(r1.at[p], sem_s1.at[p])
        wait(r2.at[p], sem_s2.at[p])
    wait(r3, sem_s3)
    wait(exr, sem_xs.at[0])
    wait(rx2, sem_xs.at[1])
    wait(rx4.at[0:15], sem_xs.at[3])


def local(tokens, key_valid, norm_gain, w_qkv, bias_table, w_proj, grad_out):
    vmem = pl.BlockSpec(memory_space=pltpu.VMEM)
    tables = make_tables()
    dma = pltpu.SemaphoreType.DMA
    result, grad_in, grad_qkv, grad_gain, grad_bias = pl.pallas_call(
        kernel,
        out_shape=(
            jax.ShapeDtypeStruct(tokens.shape, BF16),
            jax.ShapeDtypeStruct(tokens.shape, BF16),
            jax.ShapeDtypeStruct((1, 3 * D), F32),
            jax.ShapeDtypeStruct((1, D), F32),
            jax.ShapeDtypeStruct((HEADS, RELN), F32),
        ),
        in_specs=[vmem] * (7 + len(tables)),
        out_specs=[vmem] * 5,
        scratch_shapes=[
            pltpu.VMEM((24, 16, D), BF16),
            pltpu.VMEM((16, 128), F32),
            pltpu.VMEM((HEADS, RELP), F32),
            pltpu.VMEM((3, MSG, D), BF16),
            pltpu.VMEM((4, MSG, D), BF16),
            pltpu.VMEM((3, MSG, D), BF16),
            pltpu.VMEM((4, MSG, D), BF16),
            pltpu.VMEM((HEADS, WIN, WIN), F32),
            pltpu.VMEM((WIN, WIN), F32),
            pltpu.VMEM((HEADS, WIN, WIN), F32),
            pltpu.VMEM((12, WIN, 128), BF16),
            pltpu.VMEM((4, WIN, 128), BF16),
            pltpu.VMEM((WIN, D), BF16),
            pltpu.VMEM((WIN, 3 * D), BF16),
            pltpu.VMEM((PAIRS, 2, 256, CHUNK), BF16),
            pltpu.VMEM((PAIRS, 256, CHUNK), BF16),
            pltpu.VMEM((PAIRS, N_PLANE, N_Z, CHUNK), BF16),
            pltpu.VMEM((PAIRS, N_PLANE - 1, N_Z, CHUNK), BF16),
            pltpu.VMEM((N_Z, 1, 3 * D), F32),
            pltpu.VMEM((N_Z - 1, 1, 3 * D), F32),
            pltpu.VMEM((16, 8, 128), F32),
            pltpu.VMEM((7, 8, 128), F32),
            pltpu.VMEM((16, 8, 128), F32),
            pltpu.VMEM((15, 8, 128), F32),
            pltpu.VMEM((16, 8, 128), F32),
            pltpu.VMEM((16, 8, 128), F32),
            dma((3,)), dma((3,)), dma((3,)), dma((3,)),
            dma((PAIRS,)), dma((PAIRS,)), dma((PAIRS,)), dma((PAIRS,)),
            dma, dma, dma((4,)), dma((4,)),
        ],
        compiler_params=pltpu.CompilerParams(
            collective_id=0, has_side_effects=True, vmem_limit_bytes=48 * 1024 * 1024
        ),
        name="window_block",
    )(tokens, key_valid, norm_gain.reshape(1, D), w_qkv, bias_table, w_proj, grad_out, *tables)
    return result, grad_in, grad_qkv, grad_gain.reshape(D), grad_bias


def solution(mesh):
    placed = (
        P(None, "lat", "lon", None),
        P(None, "lat", "lon"),
        P(),
        P(),
        P(),
        P(),
        P(None, "lat", "lon", None),
    )
    return jax.shard_map(
        local,
        mesh=mesh,
        in_specs=placed,
        out_specs=(
            P(None, "lat", "lon", None),
            P(None, "lat", "lon", None),
            P(("lon", "lat"), None),
            P(),
            P(),
        ),
        check_vma=False,
    )
```

time: 613 us -> 74.7 us (0.12)
  the two profiles are of different devices: /device:TPU:1 before, /device:TPU:2 now
where the time goes in v1:
time: 74.7 us; the launch traced here: 74 us
  Pallas kernels  55.1 us (74%)
  local copies, waits for them, and re-layouts  18.2 us (24%)
    pallas_call x1, Pallas kernels, local(): pl.pallas_call(kernel, out_shape=(jax.ShapeDtypeStruct(tokens.shape, BF16...  55.1 us
    unnamed x34, local copies, waits for them, and re-layouts  18.2 us

profile of v1, /device:TPU:2, one launch (start us, length us, event | category | flops | bytes accessed | tf_op | source)
XLA Modules:
  0.0 74.0 jit_solution(17583085643655484287)
XLA Ops:
  0.6 0.7 copy.23.kv
  1.3 0.9 %copy.22.tok = bf16[2,6,12,512]{3,2,1,0:T(8,128)(2,1)S(1)} copy(bf16[2,6,12,512]{3,0,2,1:T(2,128)(2,1)} %param.17) | data formatting | bytes 294912 | tf_op args[0]
  2.3 0.9 %copy.24.gout = bf16[2,6,12,512]{3,2,1,0:T(8,128)(2,1)S(1)} copy(bf16[2,6,12,512]{3,0,2,1:T(2,128)(2,1)} %param.23) | data formatting | bytes 294912 | tf_op args[6]
  3.2 0.0 copy-start
  3.2 1.3 %copy-done = bf16[6,144,768]{2,1,0:T(8,128)(2,1)S(1)} copy-done((bf16[6,144,768]{2,1,0:T(8,128)(2,1)S(1)}, bf16[6,144,768]{2,1,0:T(8,128)(2,1)}, u32[]{:S(2)}) %copy-start) | copy-done | bytes 1327128
  4.5 0.0 copy-start.1
  4.5 1.0 %copy-done.1 = bf16[512,512]{1,0:T(8,128)(2,1)S(1)} copy-done((bf16[512,512]{1,0:T(8,128)(2,1)S(1)}, bf16[512,512]{1,0:T(8,128)(2,1)}, u32[]{:S(2)}) %copy-start.1) | copy-done | bytes 524312
  5.6 0.0 copy-start.2
  5.6 1.0 %copy-done.2 = bf16[512,512]{1,0:T(8,128)(2,1)S(1)} copy-done((bf16[512,512]{1,0:T(8,128)(2,1)S(1)}, bf16[512,512]{1,0:T(8,128)(2,1)}, u32[]{:S(2)}) %copy-start.2) | copy-done | bytes 524312
  6.6 0.0 copy-start.3
  6.6 1.0 %copy-done.3 = f32[2,144,144]{2,1,0:T(8,128)S(1)} copy-done((f32[2,144,144]{2,1,0:T(8,128)S(1)}, f32[2,144,144]{2,1,0:T(8,128)}, u32[]{:S(2)}) %copy-start.3) | copy-done | bytes 165912
  7.6 0.0 copy-start.4
  7.6 1.0 %copy-done.4 = bf16[384,320]{1,0:T(8,128)(2,1)S(1)} copy-done((bf16[384,320]{1,0:T(8,128)(2,1)S(1)}, bf16[384,320]{1,0:T(8,128)(2,1)}, u32[]{:S(2)}) %copy-start.4) | copy-done | bytes 245784
  8.5 0.0 copy-start.5
  8.5 0.9 %copy-done.5 = bf16[320,288]{1,0:T(8,128)(2,1)S(1)} copy-done((bf16[320,288]{1,0:T(8,128)(2,1)S(1)}, bf16[320,288]{1,0:T(8,128)(2,1)}, u32[]{:S(2)}) %copy-start.5) | copy-done | bytes 184344
  9.5 0.0 copy-start.6
  9.5 0.9 %copy-done.6 = bf16[320,384]{1,0:T(8,128)(2,1)S(1)} copy-done((bf16[320,384]{1,0:T(8,128)(2,1)S(1)}, bf16[320,384]{1,0:T(8,128)(2,1)}, u32[]{:S(2)}) %copy-start.6) | copy-done | bytes 245784
  10.4 0.0 copy-start.7
  10.4 0.9 %copy-done.7 = bf16[304,320]{1,0:T(8,128)(2,1)S(1)} copy-done((bf16[304,320]{1,0:T(8,128)(2,1)S(1)}, bf16[304,320]{1,0:T(8,128)(2,1)}, u32[]{:S(2)}) %copy-start.7) | copy-done | bytes 194584
  11.4 0.0 copy-start.8
  11.4 0.9 %copy-done.8 = f32[4,16,512]{2,1,0:T(8,128)S(1)} copy-done((f32[4,16,512]{2,1,0:T(8,128)S(1)}, f32[4,16,512]{2,1,0:T(8,128)}, u32[]{:S(2)}) %copy-start.8) | copy-done | bytes 131096
  12.3 0.0 copy-start.9
  12.3 0.9 %copy-done.9 = bf16[128,512]{1,0:T(8,128)(2,1)S(1)} copy-done((bf16[128,512]{1,0:T(8,128)(2,1)S(1)}, bf16[128,512]{1,0:T(8,128)(2,1)}, u32[]{:S(2)}) %copy-start.9) | copy-done | bytes 131096
  13.2 0.0 copy-start.10
  13.2 0.9 %copy-done.10 = s32[192,128]{1,0:T(8,128)S(1)} copy-done((s32[192,128]{1,0:T(8,128)S(1)}, s32[192,128]{1,0:T(8,128)}, u32[]{:S(2)}) %copy-start.10) | copy-done | bytes 98328
  14.1 0.0 copy-start.11
  14.1 0.7 copy-done.11
  14.8 0.0 copy-start.12
  14.8 0.7 copy-done.12
  15.5 55.1 %window_block.1 = (bf16[2,6,12,512]{3,2,1,0:T(8,128)(2,1)S(1)}, bf16[2,6,12,512]{3,2,1,0:T(8,128)(2,1)S(1)}, f32[1,1536]{1,0:T(1,128)S(1)}, f32[1,512]{1,0:T(1,128)S(1)}, f32[8,759]{1,0:T(8,128)S(1)}) custom-call(bf16[2,6,12,512]{3,2,1,0:T(8,128)(2,1)S(1)} %copy.22.tok, s32[2,6,12]{2,1,0:T(8,128)S(1)} %copy.23.kv, f32[1,512]{1,0:T(1,128)S(1)} %bitcast.2, ...), custom_call_target="tpu_custom_call" | custom-call | tf_op jit(solution)/shard_map/window_block/pallas_call | solution.py:360
  70.6 0.8 %copy.25 = bf16[2,6,12,512]{3,0,2,1:T(2,128)(2,1)} copy(bf16[2,6,12,512]{3,2,1,0:T(8,128)(2,1)S(1)} %get-tuple-element.15) | data formatting | bytes 294912
  71.4 0.8 %copy.26 = bf16[2,6,12,512]{3,0,2,1:T(2,128)(2,1)} copy(bf16[2,6,12,512]{3,2,1,0:T(8,128)(2,1)S(1)} %get-tuple-element.16) | data formatting | bytes 294912
  72.2 0.6 copy.30
  72.8 0.6 copy.31
  73.4 0.6 copy.32
Async XLA Ops:
  3.2 1.3 %copy-start = (bf16[6,144,768]{2,1,0:T(8,128)(2,1)S(1)}, bf16[6,144,768]{2,1,0:T(8,128)(2,1)}, u32[]{:S(2)}) copy-start(bf16[6,144,768]{2,1,0:T(8,128)(2,1)} %constant.27.clone.pick) | copy-start | bytes 3981316
  4.5 1.0 %copy-start.1 = (bf16[512,512]{1,0:T(8,128)(2,1)S(1)}, bf16[512,512]{1,0:T(8,128)(2,1)}, u32[]{:S(2)}) copy-start(bf16[512,512]{1,0:T(8,128)(2,1)} %w_proj.1) | copy-start | bytes 1572868
  5.6 1.0 %copy-start.2 = (bf16[512,512]{1,0:T(8,128)(2,1)S(1)}, bf16[512,512]{1,0:T(8,128)(2,1)}, u32[]{:S(2)}) copy-start(bf16[512,512]{1,0:T(8,128)(2,1)} %constant.26.clone.perm) | copy-start | bytes 1572868
  6.6 1.0 %copy-start.3 = (f32[2,144,144]{2,1,0:T(8,128)S(1)}, f32[2,144,144]{2,1,0:T(8,128)}, u32[]{:S(2)}) copy-start(f32[2,144,144]{2,1,0:T(8,128)} %constant.29.clone.masks) | copy-start | bytes 497668
  7.6 1.0 %copy-start.4 = (bf16[384,320]{1,0:T(8,128)(2,1)S(1)}, bf16[384,320]{1,0:T(8,128)(2,1)}, u32[]{:S(2)}) copy-start(bf16[384,320]{1,0:T(8,128)(2,1)} %constant.22.clone.pack_t) | copy-start | bytes 737284
  8.5 0.9 %copy-start.5 = (bf16[320,288]{1,0:T(8,128)(2,1)S(1)}, bf16[320,288]{1,0:T(8,128)(2,1)}, u32[]{:S(2)}) copy-start(bf16[320,288]{1,0:T(8,128)(2,1)} %constant.23.clone.unpack_t) | copy-start | bytes 552964
  9.5 0.9 %copy-start.6 = (bf16[320,384]{1,0:T(8,128)(2,1)S(1)}, bf16[320,384]{1,0:T(8,128)(2,1)}, u32[]{:S(2)}) copy-start(bf16[320,384]{1,0:T(8,128)(2,1)} %constant.20.clone.pack) | copy-start | bytes 737284
  10.4 0.9 %copy-start.7 = (bf16[304,320]{1,0:T(8,128)(2,1)S(1)}, bf16[304,320]{1,0:T(8,128)(2,1)}, u32[]{:S(2)}) copy-start(bf16[304,320]{1,0:T(8,128)(2,1)} %constant.21.clone.unpack) | copy-start | bytes 583684
  11.4 0.9 %copy-start.8 = (f32[4,16,512]{2,1,0:T(8,128)S(1)}, f32[4,16,512]{2,1,0:T(8,128)}, u32[]{:S(2)}) copy-start(f32[4,16,512]{2,1,0:T(8,128)} %constant.25.clone.key_row) | copy-start | bytes 393220
  12.3 0.9 %copy-start.9 = (bf16[128,512]{1,0:T(8,128)(2,1)S(1)}, bf16[128,512]{1,0:T(8,128)(2,1)}, u32[]{:S(2)}) copy-start(bf16[128,512]{1,0:T(8,128)(2,1)} %constant.24.clone.key_col) | copy-start | bytes 393220
  13.2 0.9 %copy-start.10 = (s32[192,128]{1,0:T(8,128)S(1)}, s32[192,128]{1,0:T(8,128)}, u32[]{:S(2)}) copy-start(s32[192,128]{1,0:T(8,128)} %constant.28.clone.skew_ref) | copy-start | bytes 294916
  14.1 0.7 copy-start.11
  14.8 0.7 copy-start.12

commit v2 on v1

v2 whole, which is shorter than its diff:
```python
import jax
import jax.numpy as jnp
import numpy as np
from jax import lax
from jax.experimental import pallas as pl
from jax.experimental.pallas import tpu as pltpu
from jax.sharding import PartitionSpec as P

MESH = pl.DeviceIdType.MESH
F32 = jnp.float32
BF16 = jnp.bfloat16

LEVELS, WLAT, WLON = 2, 6, 12
WIN = LEVELS * WLAT * WLON
D = 512
HEADS = 8
PAIRS = HEADS // 2
RELN = 759
RELP = 768
N_LON, N_LAT = 64, 8
N_Z = 16
N_PLANE = 16
CHUNK = 3 * 128
VMEM_LIMIT = 60 * 1024 * 1024


def offset_of(t):
    level, row, col = t // 72, t // 12 % 6, t % 12
    return 253 * level + 23 * row + col


def make_tables():
    key_col = np.zeros((128, 256), np.float32)
    key_row = np.zeros((4, 16, 256), np.float32)
    for l in range(LEVELS):
        for r in range(WLAT):
            for c in range(WLON):
                t = l * 72 + ((r + 3) % 6) * 12 + (c + 6) % 12
                key_col[c, t] = 1
                key_row[(r // 3) * 2 + c // 6, r * 2 + l, t] = 1
    perm = np.zeros((D, D), np.float32)
    for core in range(2):
        for xh in range(2):
            for lat in range(8):
                for z in range(16):
                    perm[core * 256 + (xh * 8 + lat) * 16 + z, xh * 256 + z * 16 + core * 8 + lat] = 1
    pick = np.zeros((6, WIN, RELP), np.float32)
    for g in range(6):
        for k in range(WIN):
            pick[g, k, (379 + 253 * (g // 3) + 46 * (g % 3) - offset_of(k)) % RELP] = 1
    step = np.arange(24)
    step = np.tile(23 * (step // 12) + step % 12, HEADS)
    skew = np.broadcast_to(step[:, None], (192, 128)).astype(np.int32)
    half = np.arange(WIN) // 12 % 6 >= 3
    masks = np.stack([half[:, None] != half[None, :], np.eye(WIN, dtype=bool)]).astype(np.float32)
    as_bf16 = lambda v: jnp.asarray(v, BF16)
    return (
        as_bf16(key_col),
        jnp.asarray(key_row),
        jnp.asarray(skew),
        as_bf16(pick),
        jnp.asarray(masks),
        as_bf16(perm),
    )


def dot(a, b):
    return lax.dot_general(a, b, (((1,), (0,)), ((), ())), preferred_element_type=F32)


def dot_nt(a, b):
    return lax.dot_general(a, b, (((1,), (1,)), ((), ())), preferred_element_type=F32)


def dot_tn(a, b):
    return lax.dot_general(a, b, (((0,), (0,)), ((), ())), preferred_element_type=F32)


def skewed(rows, skew, left):
    for bit in (1, 2, 4, 8, 16, 32):
        moved = pltpu.roll(rows, RELP - bit if left else bit, 1)
        rows = jnp.where((skew & bit) != 0, moved, rows)
    return rows


def window_part(ref, quad):
    return ref.at[pl.ds(3 - 3 * (quad // 2), 3), pl.ds(6 - 6 * (quad % 2), 6)]


def token_part(ref, quad):
    return ref.at[pl.ds(3 * (quad // 2), 3), pl.ds(6 * (quad % 2), 6)]


def kernel(
    tok_hbm, kv_hbm, gain_hbm, w_qkv_hbm, table_hbm, w_proj_hbm, gout_hbm,
    key_col_hbm, key_row_hbm, skew_hbm, pick_hbm, masks_hbm, perm_hbm,
    result, grad_in, qkv_hbm, dgain_hbm, dbias_hbm,
    grad_qkv, grad_gain, grad_bias, kv, gain, w_qkv, table, w_proj, key_col, key_row, skew_ref, pick, masks, perm,
    win, fin, line_up, kvs, tabs, khs, khr, bias, allowed, dscore,
    qkvs, gms, mixs, s1, r1, s2, r2, s3, r3, ex, rx2, rx3, rx4,
    sem_in, sem_own, sem_out, sem_hs, sem_hr, sem_bs, sem_br, sem_s1, sem_r1, sem_s2, sem_r2, sem_s3, sem_r3, sem_xs, sem_xr, relay,
):
    lon, lat = lax.axis_index("lon"), lax.axis_index("lat")
    xh, zc = lax.div(lon, 32), lax.rem(lon, 32)
    z, core = lax.div(zc, 2), lax.rem(zc, 2)
    plane = xh * 8 + lat
    west, east = lax.rem(lon + N_LON - 1, N_LON), lax.rem(lon + 1, N_LON)
    north, south = lax.rem(lat + N_LAT - 1, N_LAT), lax.rem(lat + 1, N_LAT)
    twin = {"lon": lon + 1 - 2 * core, "lat": lat}
    halo_to = ({"lon": west, "lat": north}, {"lon": lon, "lat": north}, {"lon": west, "lat": lat})
    back_to = ({"lon": east, "lat": south}, {"lon": lon, "lat": south}, {"lon": east, "lat": lat})

    def plane_at(d, on=core):
        other = lax.rem(plane + d, N_PLANE)
        return other, {"lon": lax.div(other, 8) * 32 + z * 2 + on, "lat": lax.rem(other, 8)}

    def z_at(d):
        other = lax.rem(z + d, N_Z)
        return other, {"lon": xh * 32 + other * 2 + core, "lat": lat}

    def far_first(i):
        return 8 + lax.div(i, 2) * (1 - 2 * lax.rem(i, 2))

    def send(src, dst, send_sem, recv_sem, to):
        pltpu.make_async_remote_copy(
            src_ref=src, dst_ref=dst, send_sem=send_sem, recv_sem=recv_sem,
            device_id=to, device_id_type=MESH,
        ).start()

    def wait(ref, sem):
        pltpu.make_async_copy(ref, ref, sem).wait()

    barrier = pltpu.get_barrier_semaphore()

    def greet(to):
        pl.semaphore_signal(barrier, inc=1, device_id=to, device_id_type=MESH)

    def greet_both(i, carry):
        greet(plane_at(i)[1])
        greet(plane_at(i, 1 - core)[1])
        return carry

    for to in halo_to + back_to + (twin,):
        greet(to)
    for d in (4, 12, 3, 13, 2, 14, 1, 15):
        greet(z_at(d)[1])
    lax.fori_loop(1, N_PLANE, greet_both, 0)

    loads = []
    for i, (src, dst) in enumerate((
        (kv_hbm, kv), (key_col_hbm, key_col), (key_row_hbm, key_row), (table_hbm, table), (skew_hbm, skew_ref),
        (pick_hbm, pick), (masks_hbm, masks), (gain_hbm, gain), (w_qkv_hbm, w_qkv), (w_proj_hbm, w_proj), (perm_hbm, perm),
    )):
        loads.append(pltpu.make_async_copy(src, dst, sem_in.at[i]))
        loads[-1].start()
    in_kv, in_key_col, in_key_row, in_table, in_skew, in_pick, in_masks, in_gain, in_w_qkv, in_w_proj, in_perm = loads
    own = [
        pltpu.make_async_copy(token_part(ref, 3), window_part(win.at[a], 3), sem_own.at[a])
        for a, ref in enumerate((tok_hbm, gout_hbm))
    ]
    for copy in own:
        copy.start()

    pl.semaphore_wait(barrier, 45)
    for quad in range(3):
        for a, ref in enumerate((tok_hbm, gout_hbm)):
            send(token_part(ref, quad), window_part(win.at[a], quad), sem_hs.at[quad, a], sem_hr.at[quad, a], halo_to[quad])
    for d in (4, 12):
        pl.semaphore_signal(relay, inc=1, device_id=z_at(d)[1], device_id_type=MESH)

    for ready in (in_kv, in_key_col, in_key_row):
        ready.wait()
    kvs[...] = jnp.zeros_like(kvs)
    for r in range(WLAT):
        kvs[r * 2 : r * 2 + 2, 0:WLON] = kv[r].astype(F32)
    keys = dot(kvs[...].astype(BF16), key_col[...])
    for quad in range(4):
        key_line = jnp.sum(keys * key_row[quad], axis=0, keepdims=True)
        if quad == 3:
            khr[3] = key_line
        else:
            khs[quad] = key_line
            send(khs.at[quad], khr.at[quad], sem_hs.at[quad, 2], sem_hr.at[quad, 2], halo_to[quad])

    for ready in (in_table, in_skew, in_pick):
        ready.wait()
    tabs[...] = jnp.zeros_like(tabs)
    tabs[:, 0:RELN] = table[...]
    skew = jnp.broadcast_to(skew_ref[:, 0:1], (192, RELP))
    rows = jnp.concatenate(
        [jnp.broadcast_to(tabs[h : h + 1, :], (24, RELP)) for h in range(HEADS)], axis=0
    )
    rows = skewed(rows, skew, True)
    high = rows.astype(BF16)
    low = (rows - high.astype(F32)).astype(BF16)
    both = jnp.concatenate([high, low], axis=0)
    for g in range(6):
        part = dot_nt(both, pick[g])
        part = part[:192] + part[192:]
        for h in range(HEADS):
            bias[h, g * 24 : (g + 1) * 24, :] = part[h * 24 : (h + 1) * 24]

    for copy in own:
        copy.wait()
    for quad in range(3):
        for a in range(2):
            wait(window_part(win.at[a], quad), sem_hr.at[quad, a])
        wait(khr.at[quad], sem_hr.at[quad, 2])
    for ready in (in_masks, in_gain, in_w_qkv, in_w_proj, in_perm):
        ready.wait()

    def gather(a):
        line_up[...] = win[a].astype(F32).reshape(8 * 72, 128)
        levels = []
        for l in range(LEVELS):
            parts = [line_up[pl.ds(2 * j + l, 72, stride=8), :] for j in range(4)]
            levels.append(jnp.concatenate(parts, axis=1))
        return jnp.concatenate(levels, axis=0)

    x = gather(0)
    cot = gather(1)
    key_ok = (khr[0] + khr[1] + khr[2] + khr[3])[:, 0:WIN]
    edge = (lat == N_LAT - 1).astype(F32)
    allowed[...] = (1.0 - edge * masks[0]) * jnp.maximum(key_ok, masks[1])

    centred = x - jnp.mean(x, axis=-1, keepdims=True)
    spread = jnp.mean(centred * centred, axis=-1, keepdims=True)
    rstd = lax.rsqrt(spread + 1e-5)
    xhat = centred * rstd
    normed = (xhat * gain[...]).astype(BF16)
    act = dot(normed, w_qkv[...]).astype(BF16)
    grad_mixed = dot_nt(cot.astype(BF16), w_proj[...]).astype(BF16)
    for j in range(12):
        qkvs[j] = act[:, j * 128 : (j + 1) * 128]
    for j in range(4):
        gms[j] = grad_mixed[:, j * 128 : (j + 1) * 128]
    normed_t = dot_nt(perm[...], normed).astype(BF16)
    first = lax.broadcasted_iota(jnp.int32, (WIN, 128), 1) < 64

    def plane_step(p):
        wait(r1.at[p], sem_r1.at[p])
        s2[p] = (s1[p, core].astype(F32) + r1[p].astype(F32)).astype(BF16).reshape(N_PLANE, N_Z, CHUNK)

        def one(i, carry):
            d = far_first(i)
            other, to = plane_at(d)
            send(s2.at[p, other], r2.at[p, d - 1], sem_s2.at[p], sem_r2.at[p], to)
            return carry

        lax.fori_loop(1, N_PLANE, one, 0)

    def table_step(p):
        part = jnp.zeros((48, RELP), F32)
        for g in range(6):
            group = jnp.concatenate([dscore[h, g * 24 : (g + 1) * 24, :] for h in (2 * p, 2 * p + 1)], axis=0)
            part = part + dot(group.astype(BF16), pick[g])
        part = skewed(part, skew[:48], False)
        for s in range(2):
            h = 2 * p + s
            line = jnp.sum(part[s * 24 : (s + 1) * 24], axis=0, keepdims=True)
            for j in range(6):
                ex[2 * j + h // 4, h % 4 : h % 4 + 1, :] = line[:, j * 128 : (j + 1) * 128]

    ex[...] = jnp.zeros_like(ex)
    grad_normed = jnp.zeros((WIN, D), F32)
    for p in range(PAIRS):
        q2, k2, v2, gm2 = qkvs[p], qkvs[4 + p], qkvs[8 + p], gms[p]
        zero = jnp.zeros_like(q2)
        mixed = dq = dk = dv = jnp.zeros((WIN, 128), F32)
        for s in range(2):
            h = 2 * p + s
            mine = first if s == 0 else jnp.logical_not(first)
            qm = jnp.where(mine, q2, zero) * jnp.asarray(0.125, BF16)
            km = jnp.where(mine, k2, zero)
            vm = jnp.where(mine, v2, zero)
            gm = jnp.where(mine, gm2, zero)
            weights = jnp.exp(dot_nt(qm, k2) + bias[h]) * allowed[...]
            probs = weights / jnp.sum(weights, axis=-1, keepdims=True)
            attention = probs.astype(BF16)
            mixed = mixed + dot(attention, vm)
            grad_att = dot_nt(gm, v2).astype(BF16).astype(F32)
            pull = probs * grad_att
            grad_scores = pull - probs * jnp.sum(pull, axis=-1, keepdims=True)
            dscore[h] = grad_scores
            short = grad_scores.astype(BF16)
            dq = dq + dot(short, km)
            dk = dk + dot_tn(short, qm)
            dv = dv + dot_tn(attention, gm)
        mixs[:, p * 128 : (p + 1) * 128] = mixed.astype(BF16)
        act_part = jnp.concatenate([(dq * 0.125).astype(BF16), dk.astype(BF16), dv.astype(BF16)], axis=1)
        s1[p] = dot(normed_t, act_part).astype(BF16).reshape(2, 256, CHUNK)
        send(s1.at[p, 1 - core], r1.at[p], sem_s1.at[p], sem_r1.at[p], twin)
        w_part = jnp.concatenate([w_qkv[:, j * D + p * 128 : j * D + (p + 1) * 128] for j in range(3)], axis=1)
        grad_normed = grad_normed + dot_nt(act_part, w_part)
        table_step(p)
        if p > 0:
            plane_step(p - 1)

    grad_normed = grad_normed.astype(BF16).astype(F32)
    gain_part = jnp.sum(grad_normed * xhat, axis=0, keepdims=True)
    for j in range(4):
        ex[12, j : j + 1, :] = gain_part[:, j * 128 : (j + 1) * 128]
    def share_plane(i, carry):
        d = far_first(i)
        other, to = plane_at(d)
        send(ex.at[other], rx2.at[d - 1], sem_xs.at[0], sem_xr.at[0], to)
        return carry

    lax.fori_loop(1, N_PLANE, share_plane, 0)
    plane_step(PAIRS - 1)

    grad_hat = grad_normed * gain[...]
    shift = jnp.mean(grad_hat, axis=-1, keepdims=True)
    slope = jnp.mean(grad_hat * xhat, axis=-1, keepdims=True)
    dx = cot + rstd * (grad_hat - shift - xhat * slope)
    out = x + dot(mixs[...], w_proj[...]).astype(BF16).astype(F32)
    own = []
    for a, (values, ref) in enumerate(((out, result), (dx, grad_in))):
        for l in range(LEVELS):
            for j in range(4):
                line_up[pl.ds(2 * j + l, 72, stride=8), :] = values[l * 72 : (l + 1) * 72, j * 128 : (j + 1) * 128]
        fin[a] = line_up[...].reshape(WLAT, WLON, 8, 128).astype(BF16)
        for quad in range(3):
            send(window_part(fin.at[a], quad), token_part(ref, quad), sem_bs.at[quad, a], sem_br.at[quad, a], back_to[quad])
        own.append(pltpu.make_async_copy(window_part(fin.at[a], 3), token_part(ref, 3), sem_own.at[a]))
        own[-1].start()

    def z_step(p):
        wait(r2.at[p], sem_r2.at[p])
        total = s2[p, plane].astype(F32)
        for d in range(N_PLANE - 1):
            total = total + r2[p, d].astype(F32)
        for row in range(N_Z):
            s3[p, row] = total[row : row + 1]

        def one(i, carry):
            d = far_first(i)
            other, to = z_at(d)
            send(s3.at[p, other], r3.at[p, d - 1], sem_s3.at[p], sem_r3.at[p], to)
            return carry

        lax.fori_loop(1, N_Z, one, 0)

    pl.semaphore_wait(relay, 2)
    z_step(0)
    z_step(1)
    wait(rx2, sem_xr.at[0])
    rx3[z] = ex[plane] + jnp.sum(rx2[...], axis=0)

    def share_z(i, carry):
        send(rx3.at[z], rx3.at[z], sem_xs.at[1], sem_xr.at[1], z_at(far_first(i))[1])
        return carry

    lax.fori_loop(1, N_Z, share_z, 0)
    z_step(2)
    z_step(3)

    wait(rx3.at[0:15], sem_xr.at[1])
    wait(rx3.at[0:15], sem_xs.at[1])
    mine = core * N_PLANE + plane
    rx4[mine] = jnp.sum(rx3[...], axis=0)

    def share_back(i, carry):
        d = far_first(i)
        send(rx4.at[mine], rx4.at[mine], sem_xs.at[2], sem_xr.at[2], plane_at(d)[1])
        send(rx4.at[mine], rx4.at[mine], sem_xs.at[2], sem_xr.at[2], plane_at(d, 1 - core)[1])
        return carry

    lax.fori_loop(1, N_PLANE, share_back, 0)
    send(rx4.at[mine], rx4.at[mine], sem_xs.at[2], sem_xr.at[2], twin)

    for p in range(PAIRS):
        wait(r3.at[p], sem_r3.at[p])
        line = s3[p, z] + jnp.sum(r3[p], axis=0)
        for j in range(3):
            grad_qkv[:, j * D + p * 128 : j * D + (p + 1) * 128] = line[:, j * 128 : (j + 1) * 128]
    own.append(pltpu.make_async_copy(grad_qkv, qkv_hbm, sem_out.at[2]))
    own[-1].start()
    wait(rx4.at[0:31], sem_xr.at[2])
    sums = rx4[0:N_PLANE] + rx4[N_PLANE : 2 * N_PLANE]
    for j in range(4):
        grad_gain[:, j * 128 : (j + 1) * 128] = sums[12, j : j + 1, :]
    for j in range(6):
        width = min(128, RELN - j * 128)
        for half in range(2):
            grad_bias[half * 4 : half * 4 + 4, j * 128 : j * 128 + width] = sums[2 * j + half, :, 0:width]
    for i, (src, dst) in enumerate(((grad_gain, dgain_hbm), (grad_bias, dbias_hbm))):
        own.append(pltpu.make_async_copy(src, dst, sem_out.at[i]))
        own[-1].start()

    for copy in own:
        copy.wait()
    for quad in range(3):
        for a, ref in enumerate((result, grad_in)):
            wait(token_part(ref, quad), sem_br.at[quad, a])
            wait(token_part(ref, quad), sem_bs.at[quad, a])
            wait(window_part(win.at[a], quad), sem_hs.at[quad, a])
        wait(khs.at[quad], sem_hs.at[quad, 2])
    for p in range(PAIRS):
        wait(r1.at[p], sem_s1.at[p])
        wait(r2.at[p], sem_s2.at[p])
        wait(r3.at[p], sem_s3.at[p])
    wait(rx2, sem_xs.at[0])
    wait(rx4.at[0:31], sem_xs.at[2])


def finish(*refs):
    ins, outs, held, sem_in, sem_out = refs[:5], refs[5:10], refs[10:15], refs[15], refs[16]
    arrivals = [pltpu.make_async_copy(src, mid, sem_in.at[i]) for i, (src, mid) in enumerate(zip(ins, held))]
    leaves = [pltpu.make_async_copy(mid, dst, sem_out.at[i]) for i, (mid, dst) in enumerate(zip(held, outs))]
    for copy in arrivals:
        copy.start()
    for arrival, leave in zip(arrivals, leaves):
        arrival.wait()
        leave.start()
    for copy in leaves:
        copy.wait()


def to_tiles(x):
    return x.transpose(1, 2, 0, 3).reshape(WLAT, WLON, LEVELS, 4, 128).transpose(0, 1, 3, 2, 4).reshape(WLAT, WLON, 8, 128)


def from_tiles(x):
    x = x.reshape(WLAT, WLON, 4, LEVELS, 128).transpose(0, 1, 3, 2, 4).reshape(WLAT, WLON, LEVELS, D)
    return x.transpose(2, 0, 1, 3)


def local(tokens, key_valid, norm_gain, w_qkv, bias_table, w_proj, grad_out):
    hbm = pl.BlockSpec(memory_space=pl.ANY)
    tables = make_tables()
    dma = pltpu.SemaphoreType.DMA
    operands = (
        to_tiles(tokens), key_valid.transpose(1, 0, 2), norm_gain.reshape(1, D), w_qkv, bias_table, w_proj, to_tiles(grad_out),
    ) + tables
    loaded = [operands[i] for i in (1, 2, 3, 4, 5)] + list(tables)
    shapes = (
        jax.ShapeDtypeStruct((WLAT, WLON, 8, 128), BF16),
        jax.ShapeDtypeStruct((WLAT, WLON, 8, 128), BF16),
        jax.ShapeDtypeStruct((1, 3 * D), F32),
        jax.ShapeDtypeStruct((1, D), F32),
        jax.ShapeDtypeStruct((HEADS, RELN), F32),
    )
    parts = pl.pallas_call(
        kernel,
        out_shape=shapes,
        in_specs=[hbm] * len(operands),
        out_specs=[hbm] * 5,
        scratch_shapes=[pltpu.VMEM(v.shape, v.dtype) for v in list(shapes[2:]) + loaded] + [
            pltpu.VMEM((2, WLAT, WLON, 8, 128), BF16),
            pltpu.VMEM((2, WLAT, WLON, 8, 128), BF16),
            pltpu.VMEM((8 * 72, 128), F32),
            pltpu.VMEM((16, 128), F32),
            pltpu.VMEM((HEADS, RELP), F32),
            pltpu.VMEM((3, 1, 256), F32),
            pltpu.VMEM((4, 1, 256), F32),
            pltpu.VMEM((HEADS, WIN, WIN), F32),
            pltpu.VMEM((WIN, WIN), F32),
            pltpu.VMEM((HEADS, WIN, WIN), F32),
            pltpu.VMEM((12, WIN, 128), BF16),
            pltpu.VMEM((4, WIN, 128), BF16),
            pltpu.VMEM((WIN, D), BF16),
            pltpu.VMEM((PAIRS, 2, 256, CHUNK), BF16),
            pltpu.VMEM((PAIRS, 256, CHUNK), BF16),
            pltpu.VMEM((PAIRS, N_PLANE, N_Z, CHUNK), BF16),
            pltpu.VMEM((PAIRS, N_PLANE - 1, N_Z, CHUNK), BF16),
            pltpu.VMEM((PAIRS, N_Z, 1, CHUNK), F32),
            pltpu.VMEM((PAIRS, N_Z - 1, 1, CHUNK), F32),
            pltpu.VMEM((16, 4, 128), F32),
            pltpu.VMEM((15, 4, 128), F32),
            pltpu.VMEM((16, 4, 128), F32),
            pltpu.VMEM((32, 4, 128), F32),
            dma((len(loaded),)), dma((2,)), dma((3,)), dma((3, 3)), dma((3, 3)), dma((3, 2)), dma((3, 2)),
            dma((PAIRS,)), dma((PAIRS,)), dma((PAIRS,)), dma((PAIRS,)),
            dma((PAIRS,)), dma((PAIRS,)), dma((3,)), dma((3,)), pltpu.SemaphoreType.REGULAR,
        ],
        compiler_params=pltpu.CompilerParams(
            collective_id=0, has_side_effects=True, vmem_limit_bytes=VMEM_LIMIT
        ),
        name="window_block",
    )(*operands)
    result, grad_in, grad_qkv, grad_gain, grad_bias = pl.pallas_call(
        finish,
        out_shape=shapes,
        in_specs=[hbm] * 5,
        out_specs=[hbm] * 5,
        scratch_shapes=[pltpu.VMEM(v.shape, v.dtype) for v in shapes] + [dma((5,)), dma((5,))],
        compiler_params=pltpu.CompilerParams(vmem_limit_bytes=VMEM_LIMIT),
        name="finish",
    )(*parts)
    return from_tiles(result), from_tiles(grad_in), grad_qkv, grad_gain.reshape(D), grad_bias


def solution(mesh):
    placed = (
        P(None, "lat", "lon", None),
        P(None, "lat", "lon"),
        P(),
        P(),
        P(),
        P(),
        P(None, "lat", "lon", None),
    )
    return jax.shard_map(
        local,
        mesh=mesh,
        in_specs=placed,
        out_specs=(
            P(None, "lat", "lon", None),
            P(None, "lat", "lon", None),
            P(("lon", "lat"), None),
            P(),
            P(),
        ),
        check_vma=False,
    )
```

time: 74.7 us -> 54.5 us (0.73)
  the two profiles are of different devices: /device:TPU:2 before, /device:TPU:1 now
where the time goes in v2:
time: 54.5 us; the launch traced here: 54.4 us
  Pallas kernels  53.7 us (99%)
  between operations  0.64 us (1%)
    pallas_call x1, Pallas kernels, local(): pl.pallas_call(kernel, out_shape=shapes, in_specs=[hbm] * len(operands),...  52 us
    pallas_call x1, Pallas kernels, local(): pl.pallas_call(finish, out_shape=shapes, in_specs=[hbm] * 5, out_specs=[h...  1.74 us

profile of v2, /device:TPU:1, one launch (start us, length us, event | category | flops | bytes accessed | tf_op | source)
XLA Modules:
  0.0 54.4 jit_solution(13563942556809529816)
XLA Ops:
  0.6 52.0 %window_block.1 = (bf16[6,12,8,128]{3,2,1,0:T(8,128)(2,1)}, bf16[6,12,8,128]{3,2,1,0:T(8,128)(2,1)}, f32[1,1536]{1,0:T(1,128)}, f32[1,512]{1,0:T(1,128)}, f32[8,759]{1,0:T(8,128)}) custom-call(bf16[6,12,8,128]{3,2,1,0:T(8,128)(2,1)} %bitcast.31, s32[6,2,12]{2,1,0:T(2,128)} %bitcast.33, f32[1,512]{1,0:T(1,128)} %bitcast.34, bf16[512,1536]{1,0:T(8,128)(2,1)} %w_qkv_hbm.1, ...), custom_call_target="tpu_custom_call" | custom-call | tf_op jit(solution)/shard_map/window_block/pallas_call | solution.py:444
  52.6 1.7 %finish.1 = (bf16[6,12,8,128]{3,2,1,0:T(8,128)(2,1)}, bf16[6,12,8,128]{3,2,1,0:T(8,128)(2,1)}, f32[1,1536]{1,0:T(1,128)}, f32[1,512]{1,0:T(1,128)}, f32[8,759]{1,0:T(8,128)}) custom-call(bf16[6,12,8,128]{3,2,1,0:T(8,128)(2,1)} %get-tuple-element.15.refs_0_, bf16[6,12,8,128]{3,2,1,0:T(8,128)(2,1)} %get-tuple-element.16.refs_1_, ...), custom_call_target="tpu_custom_call" | custom-call | tf_op jit(solution)/shard_map/finish/pallas_call | solution.py:482

commit v3 on v2

--- a/solution.py
+++ b/solution.py
@@ -104,6 +104,7 @@
     xh, zc = lax.div(lon, 32), lax.rem(lon, 32)
     z, core = lax.div(zc, 2), lax.rem(zc, 2)
     plane = xh * 8 + lat
+    x_at, y_at = lax.div(plane, 4), lax.rem(plane, 4)
     west, east = lax.rem(lon + N_LON - 1, N_LON), lax.rem(lon + 1, N_LON)
     north, south = lax.rem(lat + N_LAT - 1, N_LAT), lax.rem(lat + 1, N_LAT)
     twin = {"lon": lon + 1 - 2 * core, "lat": lat}
@@ -111,8 +112,11 @@
     back_to = ({"lon": east, "lat": south}, {"lon": lon, "lat": south}, {"lon": east, "lat": lat})
 
     def plane_at(d, on=core):
-        other = lax.rem(plane + d, N_PLANE)
-        return other, {"lon": lax.div(other, 8) * 32 + z * 2 + on, "lat": lax.rem(other, 8)}
+        slow, fast = lax.div(d, 4), lax.rem(d, 4)
+        x_to = lax.rem(x_at + slow + core * (fast - slow), 4)
+        y_to = lax.rem(y_at + fast + core * (slow - fast), 4)
+        other = x_to * 4 + y_to
+        return other, {"lon": lax.div(x_to, 2) * 32 + z * 2 + on, "lat": lax.rem(x_to, 2) * 4 + y_to}
 
     def z_at(d):
         other = lax.rem(z + d, N_Z)
@@ -286,6 +290,8 @@
             dq = dq + dot(short, km)
             dk = dk + dot_tn(short, qm)
             dv = dv + dot_tn(attention, gm)
+            if s == 0 and 0 < p < PAIRS - 1:
+                plane_step(p - 1)
         mixs[:, p * 128 : (p + 1) * 128] = mixed.astype(BF16)
         act_part = jnp.concatenate([(dq * 0.125).astype(BF16), dk.astype(BF16), dv.astype(BF16)], axis=1)
         s1[p] = dot(normed_t, act_part).astype(BF16).reshape(2, 256, CHUNK)
@@ -293,8 +299,6 @@
         w_part = jnp.concatenate([w_qkv[:, j * D + p * 128 : j * D + (p + 1) * 128] for j in range(3)], axis=1)
         grad_normed = grad_normed + dot_nt(act_part, w_part)
         table_step(p)
-        if p > 0:
-            plane_step(p - 1)
 
     grad_normed = grad_normed.astype(BF16).astype(F32)
     gain_part = jnp.sum(grad_normed * xhat, axis=0, keepdims=True)
@@ -307,6 +311,7 @@
         return carry
 
     lax.fori_loop(1, N_PLANE, share_plane, 0)
+    plane_step(PAIRS - 2)
     plane_step(PAIRS - 1)
 
     grad_hat = grad_normed * gain[...]
@@ -342,8 +347,6 @@
         lax.fori_loop(1, N_Z, one, 0)
 
     pl.semaphore_wait(relay, 2)
-    z_step(0)
-    z_step(1)
     wait(rx2, sem_xr.at[0])
     rx3[z] = ex[plane] + jnp.sum(rx2[...], axis=0)
 
@@ -352,8 +355,8 @@
         return carry
 
     lax.fori_loop(1, N_Z, share_z, 0)
-    z_step(2)
-    z_step(3)
+    for p in range(PAIRS):
+        z_step(p)
 
     wait(rx3.at[0:15], sem_xr.at[1])
     wait(rx3.at[0:15], sem_xs.at[1])

time: 54.5 us -> 52.4 us (0.961)
  Pallas kernels: 53.7 us -> 51.6 us
    pallas_call x1, Pallas kernels: 52 us -> 49.9 us  [local(): pl.pallas_call(kernel, out_shape=shapes, in_specs=[hbm] * len(operands),...]
where the time goes in v3:
time: 52.4 us; the launch traced here: 52.2 us
  Pallas kernels  51.6 us (98%)
  between operations  0.64 us (1%)
    pallas_call x1, Pallas kernels, local(): pl.pallas_call(kernel, out_shape=shapes, in_specs=[hbm] * len(operands),...  49.9 us
    pallas_call x1, Pallas kernels, local(): pl.pallas_call(finish, out_shape=shapes, in_specs=[hbm] * 5, out_specs=[h...  1.74 us

profile of v3, /device:TPU:1, one launch (start us, length us, event | category | flops | bytes accessed | tf_op | source)
XLA Modules:
  0.0 52.2 jit_solution(3506871038351407152)
XLA Ops:
  0.6 49.9 %window_block.1 = (bf16[6,12,8,128]{3,2,1,0:T(8,128)(2,1)}, bf16[6,12,8,128]{3,2,1,0:T(8,128)(2,1)}, f32[1,1536]{1,0:T(1,128)}, f32[1,512]{1,0:T(1,128)}, f32[8,759]{1,0:T(8,128)}) custom-call(bf16[6,12,8,128]{3,2,1,0:T(8,128)(2,1)} %bitcast.31, s32[6,2,12]{2,1,0:T(2,128)} %bitcast.33, f32[1,512]{1,0:T(1,128)} %bitcast.34, bf16[512,1536]{1,0:T(8,128)(2,1)} %w_qkv_hbm.1, ...), custom_call_target="tpu_custom_call" | custom-call | tf_op jit(solution)/shard_map/window_block/pallas_call | solution.py:447
  50.5 1.7 %finish.1 = (bf16[6,12,8,128]{3,2,1,0:T(8,128)(2,1)}, bf16[6,12,8,128]{3,2,1,0:T(8,128)(2,1)}, f32[1,1536]{1,0:T(1,128)}, f32[1,512]{1,0:T(1,128)}, f32[8,759]{1,0:T(8,128)}) custom-call(bf16[6,12,8,128]{3,2,1,0:T(8,128)(2,1)} %get-tuple-element.15.refs_0_, bf16[6,12,8,128]{3,2,1,0:T(8,128)(2,1)} %get-tuple-element.16.refs_1_, ...), custom_call_target="tpu_custom_call" | custom-call | tf_op jit(solution)/shard_map/finish/pallas_call | solution.py:485

commit v4 on v3

--- a/solution.py
+++ b/solution.py
@@ -253,14 +253,13 @@
 
         lax.fori_loop(1, N_PLANE, one, 0)
 
-    def table_step(p):
-        part = jnp.zeros((48, RELP), F32)
+    def table_step(heads):
+        part = jnp.zeros((24 * len(heads), RELP), F32)
         for g in range(6):
-            group = jnp.concatenate([dscore[h, g * 24 : (g + 1) * 24, :] for h in (2 * p, 2 * p + 1)], axis=0)
+            group = jnp.concatenate([dscore[h, g * 24 : (g + 1) * 24, :] for h in heads], axis=0)
             part = part + dot(group.astype(BF16), pick[g])
-        part = skewed(part, skew[:48], False)
-        for s in range(2):
-            h = 2 * p + s
+        part = skewed(part, skew[: 24 * len(heads)], False)
+        for s, h in enumerate(heads):
             line = jnp.sum(part[s * 24 : (s + 1) * 24], axis=0, keepdims=True)
             for j in range(6):
                 ex[2 * j + h // 4, h % 4 : h % 4 + 1, :] = line[:, j * 128 : (j + 1) * 128]
@@ -270,7 +269,9 @@
     for p in range(PAIRS):
         q2, k2, v2, gm2 = qkvs[p], qkvs[4 + p], qkvs[8 + p], gms[p]
         zero = jnp.zeros_like(q2)
-        mixed = dq = dk = dv = jnp.zeros((WIN, 128), F32)
+        mixed = dq = jnp.zeros((WIN, 128), F32)
+        q_t, gm_t = (q2 * jnp.asarray(0.125, BF16)).T, gm2.T
+        dk_t, dv_t = [], []
         for s in range(2):
             h = 2 * p + s
             mine = first if s == 0 else jnp.logical_not(first)
@@ -279,7 +280,7 @@
             vm = jnp.where(mine, v2, zero)
             gm = jnp.where(mine, gm2, zero)
             weights = jnp.exp(dot_nt(qm, k2) + bias[h]) * allowed[...]
-            probs = weights / jnp.sum(weights, axis=-1, keepdims=True)
+            probs = weights * (1.0 / jnp.sum(weights, axis=-1, keepdims=True))
             attention = probs.astype(BF16)
             mixed = mixed + dot(attention, vm)
             grad_att = dot_nt(gm, v2).astype(BF16).astype(F32)
@@ -288,18 +289,20 @@
             dscore[h] = grad_scores
             short = grad_scores.astype(BF16)
             dq = dq + dot(short, km)
-            dk = dk + dot_tn(short, qm)
-            dv = dv + dot_tn(attention, gm)
-            if s == 0 and 0 < p < PAIRS - 1:
+            dk_t.append(dot(q_t[s * 64 : (s + 1) * 64], short))
+            dv_t.append(dot(gm_t[s * 64 : (s + 1) * 64], attention))
+            if s == 0 and p == 1:
                 plane_step(p - 1)
         mixs[:, p * 128 : (p + 1) * 128] = mixed.astype(BF16)
-        act_part = jnp.concatenate([(dq * 0.125).astype(BF16), dk.astype(BF16), dv.astype(BF16)], axis=1)
+        act_part = jnp.concatenate([(dq * 0.125).astype(BF16), jnp.concatenate(dk_t + dv_t, axis=0).astype(BF16).T], axis=1)
         s1[p] = dot(normed_t, act_part).astype(BF16).reshape(2, 256, CHUNK)
         send(s1.at[p, 1 - core], r1.at[p], sem_s1.at[p], sem_r1.at[p], twin)
         w_part = jnp.concatenate([w_qkv[:, j * D + p * 128 : j * D + (p + 1) * 128] for j in range(3)], axis=1)
         grad_normed = grad_normed + dot_nt(act_part, w_part)
-        table_step(p)
-
+        if p == PAIRS - 2:
+            table_step(range(HEADS - 2))
+
+    table_step(range(HEADS - 2, HEADS))
     grad_normed = grad_normed.astype(BF16).astype(F32)
     gain_part = jnp.sum(grad_normed * xhat, axis=0, keepdims=True)
     for j in range(4):
@@ -311,6 +314,7 @@
         return carry
 
     lax.fori_loop(1, N_PLANE, share_plane, 0)
+    plane_step(1)
     plane_step(PAIRS - 2)
     plane_step(PAIRS - 1)
 

time: 52.4 us -> 51.4 us (0.981)
  Pallas kernels: 51.6 us -> 50.6 us
    pallas_call x1, Pallas kernels: 49.9 us -> 48.9 us  [local(): pl.pallas_call(kernel, out_shape=shapes, in_specs=[hbm] * len(operands),...]
where the time goes in v4:
time: 51.4 us; the launch traced here: 51.3 us
  Pallas kernels  50.6 us (98%)
  between operations  0.64 us (1%)
    pallas_call x1, Pallas kernels, local(): pl.pallas_call(kernel, out_shape=shapes, in_specs=[hbm] * len(operands),...  48.9 us
    pallas_call x1, Pallas kernels, local(): pl.pallas_call(finish, out_shape=shapes, in_specs=[hbm] * 5, out_specs=[h...  1.74 us

profile of v4, /device:TPU:1, one launch (start us, length us, event | category | flops | bytes accessed | tf_op | source)
XLA Modules:
  0.0 51.3 jit_solution(10589049060756918945)
XLA Ops:
  0.6 48.9 %window_block.1 = (bf16[6,12,8,128]{3,2,1,0:T(8,128)(2,1)}, bf16[6,12,8,128]{3,2,1,0:T(8,128)(2,1)}, f32[1,1536]{1,0:T(1,128)}, f32[1,512]{1,0:T(1,128)}, f32[8,759]{1,0:T(8,128)}) custom-call(bf16[6,12,8,128]{3,2,1,0:T(8,128)(2,1)} %bitcast.31, s32[6,2,12]{2,1,0:T(2,128)} %bitcast.33, f32[1,512]{1,0:T(1,128)} %bitcast.34, bf16[512,1536]{1,0:T(8,128)(2,1)} %w_qkv_hbm.1, ...), custom_call_target="tpu_custom_call" | custom-call | tf_op jit(solution)/shard_map/window_block/pallas_call | solution.py:451
  49.5 1.7 %finish.1 = (bf16[6,12,8,128]{3,2,1,0:T(8,128)(2,1)}, bf16[6,12,8,128]{3,2,1,0:T(8,128)(2,1)}, f32[1,1536]{1,0:T(1,128)}, f32[1,512]{1,0:T(1,128)}, f32[8,759]{1,0:T(8,128)}) custom-call(bf16[6,12,8,128]{3,2,1,0:T(8,128)(2,1)} %get-tuple-element.15.refs_0_, bf16[6,12,8,128]{3,2,1,0:T(8,128)(2,1)} %get-tuple-element.16.refs_1_, ...), custom_call_target="tpu_custom_call" | custom-call | tf_op jit(solution)/shard_map/finish/pallas_call | solution.py:489

commit v5 on v4

--- a/solution.py
+++ b/solution.py
@@ -146,18 +146,21 @@
 
     for to in halo_to + back_to + (twin,):
         greet(to)
-    for d in (4, 12, 3, 13, 2, 14, 1, 15):
-        greet(z_at(d)[1])
-    lax.fori_loop(1, N_PLANE, greet_both, 0)
-
     loads = []
     for i, (src, dst) in enumerate((
         (kv_hbm, kv), (key_col_hbm, key_col), (key_row_hbm, key_row), (table_hbm, table), (skew_hbm, skew_ref),
         (pick_hbm, pick), (masks_hbm, masks), (gain_hbm, gain), (w_qkv_hbm, w_qkv), (w_proj_hbm, w_proj), (perm_hbm, perm),
     )):
         loads.append(pltpu.make_async_copy(src, dst, sem_in.at[i]))
-        loads[-1].start()
     in_kv, in_key_col, in_key_row, in_table, in_skew, in_pick, in_masks, in_gain, in_w_qkv, in_w_proj, in_perm = loads
+    for load in loads[:3]:
+        load.start()
+    for d in (4, 12, 3, 13, 2, 14, 1, 15):
+        greet(z_at(d)[1])
+    lax.fori_loop(1, N_PLANE, greet_both, 0)
+
+    for load in loads[3:]:
+        load.start()
     own = [
         pltpu.make_async_copy(token_part(ref, 3), window_part(win.at[a], 3), sem_own.at[a])
         for a, ref in enumerate((tok_hbm, gout_hbm))

time: 51.4 us -> 51.4 us (level)
  no operation moved by 1% of the time
where the time goes in v5:
time: 51.4 us; the launch traced here: 51.3 us
  Pallas kernels  50.6 us (98%)
  between operations  0.64 us (1%)
    pallas_call x1, Pallas kernels, local(): pl.pallas_call(kernel, out_shape=shapes, in_specs=[hbm] * len(operands),...  48.9 us
    pallas_call x1, Pallas kernels, local(): pl.pallas_call(finish, out_shape=shapes, in_specs=[hbm] * 5, out_specs=[h...  1.74 us

profile of v5, /device:TPU:1, one launch (start us, length us, event | category | flops | bytes accessed | tf_op | source)
XLA Modules:
  0.0 51.3 jit_solution(2180334352794639216)
XLA Ops:
  0.6 48.9 %window_block.1 = (bf16[6,12,8,128]{3,2,1,0:T(8,128)(2,1)}, bf16[6,12,8,128]{3,2,1,0:T(8,128)(2,1)}, f32[1,1536]{1,0:T(1,128)}, f32[1,512]{1,0:T(1,128)}, f32[8,759]{1,0:T(8,128)}) custom-call(bf16[6,12,8,128]{3,2,1,0:T(8,128)(2,1)} %bitcast.31, s32[6,2,12]{2,1,0:T(2,128)} %bitcast.33, f32[1,512]{1,0:T(1,128)} %bitcast.34, bf16[512,1536]{1,0:T(8,128)(2,1)} %w_qkv_hbm.1, ...), custom_call_target="tpu_custom_call" | custom-call | tf_op jit(solution)/shard_map/window_block/pallas_call | solution.py:454
  49.5 1.7 %finish.1 = (bf16[6,12,8,128]{3,2,1,0:T(8,128)(2,1)}, bf16[6,12,8,128]{3,2,1,0:T(8,128)(2,1)}, f32[1,1536]{1,0:T(1,128)}, f32[1,512]{1,0:T(1,128)}, f32[8,759]{1,0:T(8,128)}) custom-call(bf16[6,12,8,128]{3,2,1,0:T(8,128)(2,1)} %get-tuple-element.15.refs_0_, bf16[6,12,8,128]{3,2,1,0:T(8,128)(2,1)} %get-tuple-element.16.refs_1_, ...), custom_call_target="tpu_custom_call" | custom-call | tf_op jit(solution)/shard_map/finish/pallas_call | solution.py:492
